TPU v7x, 128 devices: a whole 4x4x4 slice. The times are simulated.
128 devices in a mesh: gx: 8 (over x_lo, y), gy: 16 (over x_hi, z, core).
Axes of the slice: x: 4 (x_hi: 2, x_lo: 2; x = x_hi * 2 + x_lo), y: 4, z: 4, core: 2. Of those that a mesh axis runs over, the one named last changes fastest.
Arguments:
- adjoint: float32 [2, 16, 256, 2048], P(None, None, 'gx', 'gy'), may hold values from -6 to 6
- base_flow: bfloat16 [2, 16, 256, 2048], P(None, None, 'gx', 'gy'), may hold values from -3 to 3
- slot_cell: int32 [8, 16, 3, 8, 128], P('gx', 'gy'), may hold values from 0 to 3708, as said below
- slot_marker: int32 [8, 16, 3, 8, 128], P('gx', 'gy'), may hold values from 0 to 4095, as said below
- slot_count: int32 [8, 16, 3, 8], P('gx', 'gy'), may hold values from 0 to 128, as said below
- slot_weight: float32 [8, 16, 3, 8, 16, 128], P('gx', 'gy'), may hold values from 0.02 to 0.12
- marker_source: float32 [2, 16, 64, 512], P(None, 'gx', 'gy'), may hold values from -6 to 6
Outputs:
- adjoint_out: float32 [2, 16, 256, 2048], P(None, None, 'gx', 'gy')
- marker_force: float32 [2, 16, 64, 512], P(None, 'gx', 'gy')
Inputs may be any that keep to these rules, and one draw needn't show every extreme that they name: `slot_cell`: i * 128 + j with i <= 28 and j <= 124; almost every cell lies near its marker's place on the section's circle. `slot_marker`: a marker row of the owner. `slot_count`: zero where b + g - 1 lies outside 0 to 15; every tile fills all 128 slots to some owner of its own column of owners.
All inputs are finite; a program needn't handle non-finite values.
Results may differ from a plain program's by a relative error of at most 0.002.
Values may be sent and summed in bfloat16 or wider, within the bound.
No kernel may reach another device: no remote copies, remote signals or barrier semaphores. Data moves between devices by JAX's collectives and lax.ppermute only.
A program may use at most 128 MiB of HBM per device.

v0:
```python
import functools

import jax
import jax.numpy as jnp
from jax import lax
from jax.experimental import pallas as pl
from jax.experimental.pallas import tpu as pltpu
from jax.sharding import Mesh, PartitionSpec as P

SUBSTEPS = 3
SWEEPS = 8

TIME_STEP = 0.5
VISCOSITY = 0.2
STIFFNESS = 2.0
BENDING = 0.25

F32 = jnp.float32
BF16 = jnp.bfloat16
I32 = jnp.int32

GX = 8
ROWS = 32
COLS = 128
NROW = GX * ROWS
NCOL = 2 * COLS
LAST = 7
RIM = 16
STRIP = 2 * RIM
THIN = 8
KEPT = 192
PACK = 304
SPAN = 128
TILES = 2 * GX
DEPTH = 3
EMPTY = TILES * DEPTH
COUNT_AT = 127
GROUP = 12

NT = (((1,), (1,)), ((), ()))
NN = (((1,), (0,)), ((), ()))

PARAMS = pltpu.CompilerParams(vmem_limit_bytes=24 * 1024 * 1024)
ROOMY = pltpu.CompilerParams(vmem_limit_bytes=60 * 1024 * 1024)
VMEM = pl.BlockSpec(memory_space=pltpu.VMEM)
SMEM = pl.BlockSpec(memory_space=pltpu.SMEM)
HBM = pl.BlockSpec(memory_space=pltpu.HBM)


def call(body, outs, ins, scratch=(), spaces=(), out_specs=None, params=PARAMS):
    spaces = dict(spaces)
    return pl.pallas_call(
        body,
        out_shape=outs,
        in_specs=[spaces.get(n, VMEM) for n in range(len(ins))],
        out_specs=out_specs or jax.tree.map(lambda _: VMEM, outs),
        scratch_shapes=list(scratch),
        compiler_params=params,
    )(*ins)


OUTER_SCRATCH = (
    pltpu.VMEM((TILES, 8 * ROWS, 2 * COLS), BF16),
    pltpu.VMEM((COLS, 2 * KEPT), F32),
) + tuple(pltpu.VMEM((8 * ROWS, SPAN), F32) for _ in range(GROUP))
SPREAD_SCRATCH = (
    pltpu.VMEM((KEPT, 2 * COLS), BF16),
    pltpu.VMEM((TILES, 8 * ROWS, COLS), F32),
)


def shape(*dims, dtype=F32):
    return jax.ShapeDtypeStruct(dims, dtype)


def exchanged(far, near, step=1):
    count = lax.axis_size("zc")
    ups = [(n, (n + step) % count) for n in range(count)]
    results = []
    for value, parity in ((far, 1), (near, 0)):
        pairs = [pair for pair in ups if (pair[0] // step) % 2 == parity]
        pairs = pairs + [(target, source) for source, target in pairs]
        results.append(lax.ppermute(value, "zc", pairs))
    return results


def swapped(value):
    return lax.ppermute(value, "xh", [(0, 1), (1, 0)])


def two_parts(value):
    high = value.astype(BF16)
    return high, (value - high.astype(F32)).astype(BF16)


def row_next(x):
    lane = lax.broadcasted_iota(I32, x.shape, 1)
    return jnp.where(lane == NROW - 1, 0.0, pltpu.roll(x, NROW - 1, 1))


def row_prev(x):
    lane = lax.broadcasted_iota(I32, x.shape, 1)
    return jnp.where(lane == 0, 0.0, pltpu.roll(x, 1, 1))


def col_next(x):
    return pltpu.roll(x, x.shape[0] - 1, 0)


def col_prev(x):
    return pltpu.roll(x, 1, 0)


def pack_kernel(
    count_hbm, adj_hbm, base_hbm, cell_hbm, mark_hbm, weight_hbm, out_ref,
    count_ref, adj_ref, base_ref, cell_ref, mark_ref, weight_ref, sems,
):
    copies = [
        pltpu.make_async_copy(src, dst, sems.at[n])
        for n, (src, dst) in enumerate(
            (
                (cell_hbm, cell_ref),
                (mark_hbm, mark_ref),
                (weight_hbm, weight_ref),
                (base_hbm, base_ref),
                (adj_hbm, adj_ref),
                (count_hbm, count_ref),
            )
        )
    ]
    for copy in copies:
        copy.start()
    copies[5].wait()
    copies[0].wait()
    copies[1].wait()
    lane = lax.broadcasted_iota(I32, (1, COLS), 1)
    none = jnp.zeros((4, COLS), F32)
    for e in range(GX):
        for q in range(2):
            rows = []
            for g in range(3):
                cell = cell_ref[g, e : e + 1, :]
                mark = mark_ref[g, e : e + 1, :]
                live = (lane < count_ref[0, 0, g, e]) & ((mark >> 11) == q)
                rows += [cell >> 7, cell & 127, jnp.where(live, (mark >> 7) & 15, -1), mark & 127]
            ints = jnp.concatenate([r.astype(F32) for r in rows] + [none], axis=0)
            out_ref[2 * e + q, 288:304, :] = ints.astype(BF16)
    copies[2].wait()
    for e in range(GX):
        for g in range(3):
            hi, lo = two_parts(weight_ref[g, e])
            for q in range(2):
                out_ref[2 * e + q, 192 + 16 * g : 208 + 16 * g, :] = hi
                out_ref[2 * e + q, 240 + 16 * g : 256 + 16 * g, :] = lo
    copies[3].wait()
    for p in range(2 * GX):
        for c in range(2):
            out_ref[p, 128 + c * ROWS : 128 + (c + 1) * ROWS, :] = base_ref[c, p]
    copies[4].wait()
    for p in range(2 * GX):
        for c in range(2):
            hi, lo = two_parts(adj_ref[c, p])
            out_ref[p, c * ROWS : (c + 1) * ROWS, :] = hi
            out_ref[p, 64 + c * ROWS : 64 + (c + 1) * ROWS, :] = lo


def closed_up(blocks):
    lane = lax.broadcasted_iota(I32, (1, 1, SPAN), 2)
    spot = lax.broadcasted_iota(I32, (1, 24, SPAN), 1)
    blank = jnp.where(spot == 20, -1.0, 0.0)
    for bit in range(9):
        step = 1 << bit
        goes = []
        stays = []
        for x in blocks:
            away = x[:, 20:21, :].astype(I32)
            flag = (away >> bit) & 1
            goes.append(jnp.where((away >= 0) & (flag == 1), 1.0, 0.0))
            stays.append((away >= 0) & (flag == 0))

        def ahead(values, n):
            if step >= SPAN:
                m = n + step // SPAN
                return values[m] if m < len(values) else None
            here = pltpu.roll(values[n], SPAN - step, 2)
            if n + 1 < len(values):
                there = pltpu.roll(values[n + 1], SPAN - step, 2)
            else:
                there = jnp.zeros_like(here)
            return jnp.where(lane < SPAN - step, here, there)

        result = []
        for n, x in enumerate(blocks):
            kept = jnp.where(stays[n], x, blank)
            coming = ahead(goes, n)
            if coming is None:
                result.append(kept)
            else:
                result.append(jnp.where(coming > 0.5, ahead(blocks, n), kept))
        blocks = result
    return blocks


def unpack_kernel(place_ref, got_ref, source_ref, adj_ref, base_ref, far_ref, near_ref):
    place = place_ref[0]
    for n in range(4):
        for side in range(2):
            parts = []
            for a in range(GX):
                d = 2 * a + side
                at = (n % 2) * ROWS
                if n < 2:
                    part = got_ref[d, at : at + ROWS, :].astype(F32)
                    part = part + got_ref[d, 64 + at : 64 + at + ROWS, :].astype(F32)
                else:
                    part = got_ref[d, 128 + at : 128 + at + ROWS, :].astype(F32)
                parts.append(part)
            turned = jnp.concatenate(parts, axis=0).T
            ref = adj_ref if n < 2 else base_ref
            ref[n % 2, side * COLS : (side + 1) * COLS, :] = turned
            far_ref[side, n], near_ref[side, n] = turned_round(
                place, turned[:THIN], turned[COLS - THIN :]
            )
    for c in range(2):
        for side in range(2):
            both = jnp.concatenate(
                [source_ref[c, side, 0:8, :], source_ref[c, side, 8:16, :]], axis=1
            )
            far_ref[side, 4 + c] = both
            near_ref[side, 4 + c] = both


def slots_kernel(got_ref, ints_ref, weight_ref, table_ref):
    ints = got_ref[:, 288:304, :].astype(F32)
    across = lax.broadcasted_iota(I32, (SPAN, SPAN), 0) <= lax.broadcasted_iota(
        I32, (SPAN, SPAN), 1
    )
    across = jnp.where(across, 1.0, 0.0).astype(BF16)
    live = []
    ranks = []
    total = jnp.zeros((TILES, SPAN), F32)
    for g in range(3):
        alive = jnp.where(ints[:, 4 * g + 2, :] >= 0.0, 1.0, 0.0)
        bits = alive.astype(BF16)
        live.append(alive)
        ranks.append(
            total + lax.dot_general(bits, across, NN, preferred_element_type=F32)
        )
        total = total + lax.dot_general(
            bits, jnp.ones((SPAN, SPAN), BF16), NN, preferred_element_type=F32
        )
    filled = jnp.int32(0)
    here = [
        (jnp.max(total[d : d + 1]).astype(I32) + SPAN - 1) // SPAN for d in range(TILES)
    ]
    for d in range(TILES):
        for n in range(DEPTH):

            @pl.when(n < here[d])
            def _():
                table_ref[filled + n] = d * DEPTH + n

        filled = filled + here[d]
    for n in range(GROUP):
        table_ref[filled + n] = EMPTY
    table_ref[COUNT_AT] = filled
    lane = lax.broadcasted_iota(I32, (TILES, SPAN), 1).astype(F32)
    spot = lax.broadcasted_iota(I32, (TILES, 8, SPAN), 1)
    side = (lax.broadcasted_iota(I32, (TILES, 1, SPAN), 0) & 1).astype(F32)
    blocks = []
    for g in range(3):
        away = jnp.where(live[g] > 0.5, lane + float(g * SPAN + 1) - ranks[g], -1.0)
        weights = got_ref[:, 192 + 16 * g : 208 + 16 * g, :].astype(F32)
        weights = weights + got_ref[:, 240 + 16 * g : 256 + 16 * g, :].astype(F32)
        rows = [ints[:, 4 * g + n : 4 * g + n + 1, :] for n in range(4)]
        rows[2] = rows[2] + 48.0 * side + float(16 * g)
        rest = jnp.zeros((TILES, 8, SPAN), F32)
        for n, row in enumerate(rows + [away[:, None, :]]):
            rest = jnp.where(spot == n, row, rest)
        blocks.append(jnp.concatenate([weights, rest], axis=1))
    for n, block in enumerate(closed_up(blocks)):
        for d in range(TILES):
            weight_ref[d * DEPTH + n] = block[d, :16]
            ints_ref[d * DEPTH + n] = block[d, 16:].astype(I32)
    weight_ref[EMPTY] = jnp.zeros((16, SPAN), F32)
    ints_ref[EMPTY] = jnp.zeros((8, SPAN), I32)


def one_hot(index, count):
    spot = lax.broadcasted_iota(I32, (count, index.shape[1]), 0)
    return jnp.where(spot == index, 1.0, 0.0).astype(BF16)


def row_weights(first_row, weights):
    off = lax.broadcasted_iota(I32, (ROWS, SPAN), 0) - first_row
    hits = [off == n for n in range(4)]
    tables = []
    for dj in range(4):
        table = jnp.zeros((ROWS, SPAN), F32)
        for di in (3, 2, 1, 0):
            row = weights[4 * di + dj : 4 * di + dj + 1]
            table = jnp.where(hits[di], row, table)
        tables.append(table)
    return tables


def over_blocks(table_ref, body):
    def run(n, carry):
        ids = [table_ref[GROUP * n + m] for m in range(GROUP)]
        body(ids, [jnp.minimum(block // DEPTH, TILES - 1) for block in ids])
        return carry

    lax.fori_loop(0, (table_ref[COUNT_AT] + GROUP - 1) // GROUP, run, 0)


def joined(ref, ids, row):
    return jnp.concatenate([ref[block, row : row + 1, :] for block in ids], axis=1)


def turned_round(place, one, other):
    odd = (place & 1) == 1
    return jnp.where(odd, other, one), jnp.where(odd, one, other)


def neighbours(place):
    return jnp.where(place == 0, 0.0, 1.0), jnp.where(place == LAST, 0.0, 1.0)


def meeting(place, low, high, reach=1):
    start = place < reach
    end = place > LAST - reach
    has_low = jnp.where(start, 0.0, 1.0)
    has_high = jnp.where(end, 0.0, 1.0)
    lows = (low[0] * has_low, jnp.where(start, low[0], low[1]))
    highs = (jnp.where(end, high[1], high[0]), high[1] * has_high)
    return lows, highs


def masked(place):
    has_low, has_high = neighbours(place)

    def inside(x):
        width = x.shape[0]
        return jnp.concatenate(
            [x[:RIM] * has_low, x[RIM : width - RIM], x[width - RIM :] * has_high], axis=0
        )

    return inside


def projected(wide, inside, looped=False):
    div = 0.5 * (row_next(wide[0]) - row_prev(wide[0])) + 0.5 * (
        col_next(wide[1]) - col_prev(wide[1])
    )
    pressure = inside(-0.25 * div)

    def sweep(_, p):
        return inside(0.25 * (row_next(p) + row_prev(p) + col_next(p) + col_prev(p) - div))

    if looped:
        pressure = lax.fori_loop(0, SWEEPS - 1, sweep, pressure)
    else:
        for n in range(SWEEPS - 1):
            pressure = sweep(n, pressure)
    first = wide[0] - 0.5 * (row_next(pressure) - row_prev(pressure))
    second = wide[1] - 0.5 * (col_next(pressure) - col_prev(pressure))
    return inside(first), inside(second)


def strips(lows, highs, mid_ref, c):
    parts = []
    for side in range(2):
        at = side * COLS
        if mid_ref is None:
            inner = [jnp.zeros((RIM, NROW), F32)] * 2
        else:
            inner = [
                mid_ref[c, at : at + RIM, :],
                mid_ref[c, at + COLS - RIM : at + COLS, :],
            ]
        parts += [lows[side], inner[0], inner[1], highs[side]]
    return jnp.concatenate(parts, axis=0)


def rim_strips(place, far_ref, near_ref):
    result = []
    for c in range(2):
        pairs = [
            turned_round(place, far_ref[side, c].astype(F32), near_ref[side, c].astype(F32))
            for side in range(2)
        ]
        result.append(strips(*meeting(place, *zip(*pairs)), None, c))
    return result


def thin_rims(place, far, near, at):
    pairs = [turned_round(place, far[side, at], near[side, at]) for side in range(2)]
    return meeting(place, *zip(*pairs))


def outer_columns(x, side):
    at = side * 2 * STRIP
    return x[at + RIM : at + 2 * RIM], x[at + STRIP : at + STRIP + RIM]


def widened(mid_ref, c, lows, highs):
    parts = []
    for side in range(2):
        parts += [lows[side], mid_ref[c, side * COLS : (side + 1) * COLS, :], highs[side]]
    return jnp.concatenate(parts, axis=0)


def wide_projected(place, mid_ref):
    blank = (jnp.zeros((RIM, NROW), F32),) * 2
    wide = [widened(mid_ref, c, blank, blank) for c in range(2)]
    return projected(wide, masked(place), looped=True)


def transported(w, base):
    ux = 0.5 * (row_next(base[0]) - row_prev(base[0]))
    vx = 0.5 * (row_next(base[1]) - row_prev(base[1]))
    uy = 0.5 * (col_next(base[0]) - col_prev(base[0]))
    vy = 0.5 * (col_next(base[1]) - col_prev(base[1]))
    mixed = (ux * w[0] + vx * w[1], uy * w[0] + vy * w[1])
    out = []
    for c in range(2):
        east, west = row_next(w[c]), row_prev(w[c])
        north, south = col_next(w[c]), col_prev(w[c])
        laplace = east + west + north + south - 4.0 * w[c]
        value = w[c] + TIME_STEP * (
            base[0] * (0.5 * (east - west))
            + base[1] * (0.5 * (north - south))
            - mixed[c]
            + VISCOSITY * laplace
        )
        out.append(value)
    return out


def interpolate(table_ref, ints_ref, weight_ref, pick_ref, got_refs, sum_ref):
    def blocks(ids, tiles):
        for block, tile, got_ref in zip(ids, tiles, got_refs):
            cols = one_hot(ints_ref[block, 1:2, :], COLS)
            got_ref[...] = lax.dot_general(
                pick_ref[tile],
                jnp.concatenate([cols, cols], axis=0),
                NN,
                preferred_element_type=F32,
            )
        values = []
        for block, got_ref in zip(ids, got_refs):
            tables = row_weights(ints_ref[block, 0:1, :], weight_ref[block])
            both = []
            for c in range(2):
                total = jnp.zeros((ROWS, SPAN), F32)
                for dj in range(4):
                    at = (dj * 2 + c) * ROWS
                    total = total + tables[dj] * got_ref[at : at + ROWS, :]
                both.append(jnp.sum(total, axis=0, keepdims=True))
            values.append(both)
        high = lax.broadcasted_iota(I32, (96, len(ids) * SPAN), 0) == joined(ints_ref, ids, 2)
        parts = [two_parts(jnp.concatenate([v[c] for v in values], axis=1)) for c in range(2)]
        stacked = jnp.concatenate(
            [
                jnp.where(high, parts[c][k].astype(F32), 0.0).astype(BF16)
                for k in range(2)
                for c in range(2)
            ],
            axis=0,
        )
        both = lax.dot_general(
            one_hot(joined(ints_ref, ids, 3), COLS), stacked, NT, preferred_element_type=F32
        )
        sum_ref[...] = sum_ref[...] + both

    sum_ref[...] = jnp.zeros(sum_ref.shape, F32)
    over_blocks(table_ref, blocks)


def pick(field, c, side, pick_ref):
    for dj in range(4):
        shifted = pltpu.roll(field, COLS - dj, 1) if dj else field
        both = jnp.concatenate(two_parts(shifted), axis=1)
        at = (dj * 2 + c) * ROWS
        for a in range(GX):
            pick_ref[2 * a + side, at : at + ROWS, :] = both[a * ROWS : (a + 1) * ROWS]


def first_inner_kernel(mid_ref, base_ref, moved_ref):
    w = [mid_ref[c] for c in range(2)]
    out = transported(w, [base_ref[c] for c in range(2)])
    for c in range(2):
        moved_ref[c] = out[c]


def inner_kernel(place_ref, mid_ref, base_far_ref, base_ref, base_near_ref, moved_ref):
    place = place_ref[0]
    extra = RIM - THIN
    length = COLS + 2 * RIM
    w = [
        jnp.concatenate([x[extra : length - extra], x[length + extra : 2 * length - extra]], axis=0)
        for x in wide_projected(place, mid_ref)
    ]
    base = [
        widened(base_ref, c, *thin_rims(place, base_far_ref, base_near_ref, 2 + c))
        for c in range(2)
    ]
    out = transported(w, base)
    for c in range(2):
        for side in range(2):
            at = side * (COLS + 2 * THIN) + THIN
            moved_ref[c, side * COLS : (side + 1) * COLS, :] = out[c][at : at + COLS]


def outer_kernel(
    first, place_ref, table_ref, far_ref, mid_ref, near_ref, base_far_ref, base_ref,
    base_near_ref, ints_ref, weight_ref, inner_ref, moved_ref, own_ref, part_far, part_near,
    next_far, next_near, pick_ref, sum_ref, *got_refs,
):
    place = place_ref[0]
    blank = jnp.zeros((RIM - THIN, NROW), F32)

    def thin_strips(far, mid, near, c, at):
        lows, highs = thin_rims(place, far, near, at + c)
        return strips(
            [jnp.concatenate([blank, x], axis=0) for x in lows],
            [jnp.concatenate([x, blank], axis=0) for x in highs],
            mid,
            c,
        )

    base = [thin_strips(base_far_ref, base_ref, base_near_ref, c, 2) for c in range(2)]
    if first:
        w = [thin_strips(far_ref, mid_ref, near_ref, c, 0) for c in range(2)]
    else:
        w = projected(rim_strips(place, far_ref, near_ref), masked(place))
    out = transported(w, base)
    spot = lax.broadcasted_iota(I32, (RIM, NROW), 0)
    for c in range(2):
        for side in range(2):
            low, high = outer_columns(out[c], side)
            at = side * COLS
            old_low = inner_ref[c, at : at + RIM, :]
            old_high = inner_ref[c, at + COLS - RIM : at + COLS, :]
            if first:
                low = jnp.where(spot == 0, low, old_low)
                high = jnp.where(spot == RIM - 1, high, old_high)
            else:
                low = old_low + low
                high = old_high + high
            moved = jnp.concatenate(
                [low, inner_ref[c, at + RIM : at + COLS - RIM, :], high], axis=0
            )
            moved_ref[c, at : at + COLS, :] = moved
            pick(moved.T, c, side, pick_ref)
    interpolate(table_ref, ints_ref, weight_ref, pick_ref, got_refs, sum_ref)
    sums = sum_ref[...].T
    sums = sums[:KEPT] + sums[KEPT:]
    for c in range(2):
        for side in range(2):
            at = (2 * c + side) * 48
            one = sums[at : at + 48]
            own_ref[c, side] = one
            part_far[side, c], part_near[side, c] = turned_round(place, one[:32], one[16:])
            next_far[side, c], next_near[side, c] = turned_round(place >> 1, one[:16], one[32:])


def tables_kernel(table_ref, ints_ref, weight_ref, rows_ref, cols_ref):
    def blocks(ids, tiles):
        for block in ids:
            rows_ref[block] = jnp.concatenate(
                row_weights(ints_ref[block, 0:1, :], weight_ref[block]), axis=0
            )
            spot = lax.broadcasted_iota(I32, (COLS, SPAN), 0)
            hits = jnp.where(spot == ints_ref[block, 1:2, :], 1.0, 0.0).T.astype(BF16)
            cols_ref[block] = jnp.concatenate([hits, hits], axis=0)

    rows_ref[EMPTY] = jnp.zeros((4 * ROWS, SPAN), F32)
    cols_ref[EMPTY] = jnp.zeros((2 * SPAN, COLS), BF16)
    over_blocks(table_ref, blocks)


def force_of(sums, source):
    row = lax.broadcasted_iota(I32, sums.shape, 0) & 3
    lane = lax.broadcasted_iota(I32, sums.shape, 1)
    count = sums.shape[0]
    up = jnp.where(row == 0, pltpu.roll(sums, count - 3, 0), pltpu.roll(sums, 1, 0))
    down = jnp.where(row == 3, pltpu.roll(sums, 3, 0), pltpu.roll(sums, count - 1, 0))
    before = jnp.where(lane == 0, pltpu.roll(up, 1, 1), pltpu.roll(sums, 1, 1))
    after = jnp.where(lane == 127, pltpu.roll(down, 127, 1), pltpu.roll(sums, 127, 1))
    bent = before + after - 2.0 * sums
    return STIFFNESS * (sums + source - BENDING * bent)


def spread_kernel(
    place_ref, table_ref, sums_ref, beyond_far, beyond_near, from_far, from_near, thin_far,
    source_ref, thin_near, moved_ref, ints_ref, row_ref, col_ref, out_ref, edge_far, edge_near, own_ref,
    force_ref, acc_ref,
):
    place = place_ref[0]

    def unfolded(ref, side, c):
        return jnp.concatenate([ref[side, 4 + c, :, :COLS], ref[side, 4 + c, :, COLS:]], axis=0)

    for c in range(2):
        pairs = [turned_round(place, from_far[s, c], from_near[s, c]) for s in range(2)]
        lows, highs = meeting(place, *zip(*pairs))
        pairs = [turned_round(place >> 1, beyond_far[s, c], beyond_near[s, c]) for s in range(2)]
        lows2, highs2 = meeting(place, *zip(*pairs), reach=2)
        pairs = [
            turned_round(place, unfolded(thin_far, s, c), unfolded(thin_near, s, c))
            for s in range(2)
        ]
        source_lows, source_highs = meeting(place, *zip(*pairs))
        for side in range(2):
            sums = sums_ref[c, side] + jnp.concatenate(
                [
                    lows[side][:16] + lows2[side],
                    lows[side][16:] + highs[side][:16],
                    highs[side][16:] + highs2[side],
                ],
                axis=0,
            )
            source = jnp.concatenate(
                [source_lows[side], source_ref[c, side], source_highs[side]], axis=0
            )
            force = force_of(sums, source)
            own_ref[c, side] = force[16:32]
            at = (2 * c + side) * 48
            force_ref[at : at + 48, :] = jnp.concatenate(two_parts(force), axis=1)
    acc_ref[...] = jnp.zeros(acc_ref.shape, F32)

    def blocks(ids, tiles):
        spots = one_hot(joined(ints_ref, ids, 3), COLS)
        picked = lax.dot_general(
            force_ref[...], jnp.concatenate([spots, spots], axis=0), NN,
            preferred_element_type=F32,
        )
        high = lax.broadcasted_iota(I32, (96, len(ids) * SPAN), 0) == joined(ints_ref, ids, 2)
        forces = [
            TIME_STEP
            * jnp.sum(jnp.where(high, picked[96 * c : 96 * c + 96], 0.0), axis=0, keepdims=True)
            for c in range(2)
        ]
        sums = []
        for m, block in enumerate(ids):
            lanes = slice(m * SPAN, (m + 1) * SPAN)
            weighted = jnp.concatenate(
                [row_ref[block] * forces[c][:, lanes] for c in range(2)], axis=0
            )
            sums.append(
                lax.dot_general(
                    jnp.concatenate(two_parts(weighted), axis=1),
                    col_ref[block],
                    NN,
                    preferred_element_type=F32,
                )
            )
        for tile, one in zip(tiles, sums):
            acc_ref[tile] = acc_ref[tile] + one

    over_blocks(table_ref, blocks)
    for c in range(2):
        for side in range(2):
            rows = []
            for a in range(GX):
                total = jnp.zeros((ROWS, COLS), F32)
                for dj in range(4):
                    at = (4 * c + dj) * ROWS
                    one = acc_ref[2 * a + side, at : at + ROWS, :]
                    total = total + (pltpu.roll(one, dj, 1) if dj else one)
                rows.append(total)
            cols = slice(side * COLS, (side + 1) * COLS)
            total = moved_ref[c, cols, :] + jnp.concatenate(rows, axis=0).T
            out_ref[c, cols, :] = total
            far, near = turned_round(place, total[:RIM], total[COLS - RIM :])
            edge_far[side, c] = far.astype(BF16)
            edge_near[side, c] = near.astype(BF16)


def finish_inner_kernel(place_ref, mid_ref, out_ref):
    w = wide_projected(place_ref[0], mid_ref)
    for c in range(2):
        for side in range(2):
            at = side * (COLS + 2 * RIM) + RIM
            block = w[c][at : at + COLS].T
            for a in range(GX):
                out_ref[2 * a + side, c] = block[a * ROWS : (a + 1) * ROWS]


def finish_outer_kernel(place_ref, far_ref, near_ref, inner_ref, out_ref):
    place = place_ref[0]
    w = projected(rim_strips(place, far_ref, near_ref), masked(place))
    blank = jnp.zeros((COLS - 2 * RIM, NROW), F32)
    for c in range(2):
        for side in range(2):
            low, high = outer_columns(w[c], side)
            both = jnp.concatenate([low, blank, high], axis=0).T
            for a in range(GX):
                out_ref[2 * a + side, c] = (
                    inner_ref[2 * a + side, c] + both[a * ROWS : (a + 1) * ROWS]
                )


def on_device(adjoint, base_flow, slot_cell, slot_marker, slot_count, slot_weight, marker_source):
    place = lax.axis_index("zc").astype(I32).reshape(1)
    half = lax.axis_index("xh")
    whole = ("gx", "xh")
    tiles = marker_source.reshape(2, 2, 16, COLS)
    kept = lax.dynamic_index_in_dim(tiles, half, axis=1, keepdims=False)
    other = swapped(lax.dynamic_index_in_dim(tiles, 1 - half, axis=1, keepdims=False))
    source = jnp.where(
        half == 0, jnp.stack([kept, other], axis=1), jnp.stack([other, kept], axis=1)
    )
    packed = call(
        pack_kernel,
        shape(2 * GX, PACK, COLS, dtype=BF16),
        (slot_count, adjoint, base_flow, slot_cell[0, 0], slot_marker[0, 0], slot_weight[0, 0]),
        scratch=(
            pltpu.SMEM((1, 1, 3, GX), I32),
            pltpu.VMEM(adjoint.shape, F32),
            pltpu.VMEM(base_flow.shape, BF16),
            pltpu.VMEM((3, GX, COLS), I32),
            pltpu.VMEM((3, GX, COLS), I32),
            pltpu.VMEM((3, GX, 16, COLS), F32),
            pltpu.SemaphoreType.DMA((6,)),
        ),
        spaces={n: HBM for n in range(6)},
        params=ROOMY,
    )
    got = lax.all_to_all(packed, whole, split_axis=0, concat_axis=0, tiled=True)
    field = shape(2, NCOL, NROW)
    thin = shape(2, 6, THIN, NROW)
    current, base, thin_far, thin_near = call(
        unpack_kernel, (field, field, thin, thin), (place, got, source), spaces={0: SMEM}
    )
    base_far, base_near = exchanged(thin_far, thin_near)
    ints, weights, table = call(
        slots_kernel,
        (
            shape(EMPTY + 1, 8, SPAN, dtype=I32),
            shape(EMPTY + 1, 16, SPAN),
            shape(128, dtype=I32),
        ),
        (got,),
        out_specs=(VMEM, VMEM, SMEM),
    )
    far, near = base_far, base_near
    part = shape(2, 2, 32, COLS)
    beyond = shape(2, 2, 16, COLS)
    rim = shape(2, 2, RIM, NROW, dtype=BF16)
    forces = source
    row_tables = col_tables = None
    for substep in range(SUBSTEPS):
        if substep == 0:
            inner = call(first_inner_kernel, field, (current, base))
        else:
            inner = call(
                inner_kernel,
                field,
                (place, current, base_far, base, base_near),
                spaces={0: SMEM},
            )
        moved, sums, part_far, part_near, next_far, next_near = call(
            functools.partial(outer_kernel, substep == 0),
            (field, shape(2, 2, 48, COLS), part, part, beyond, beyond),
            (place, table, far, current, near, base_far, base, base_near, ints, weights, inner),
            scratch=OUTER_SCRATCH,
            spaces={0: SMEM, 1: SMEM},
        )
        beyond_far, beyond_near = exchanged(next_far, next_near, 2)
        from_far, from_near = exchanged(part_far, part_near)
        if substep == 0:
            row_tables, col_tables = call(
                tables_kernel,
                (
                    shape(EMPTY + 1, 4 * ROWS, SPAN),
                    shape(EMPTY + 1, 2 * SPAN, COLS, dtype=BF16),
                ),
                (table, ints, weights),
                spaces={0: SMEM},
            )
        current, edge_far, edge_near, forces = call(
            spread_kernel,
            (field, rim, rim, shape(2, 2, 16, COLS)),
            (
                place, table, sums, beyond_far, beyond_near, from_far, from_near, base_far,
                source, base_near, moved, ints, row_tables, col_tables,
            ),
            scratch=SPREAD_SCRATCH,
            spaces={0: SMEM, 1: SMEM},
        )
        far, near = exchanged(edge_far, edge_near)
    tiles_out = shape(2 * GX, 2, ROWS, COLS)
    inner = call(finish_inner_kernel, tiles_out, (place, current), spaces={0: SMEM})
    done = call(finish_outer_kernel, tiles_out, (place, far, near, inner), spaces={0: SMEM})
    back = lax.all_to_all(done, whole, split_axis=0, concat_axis=0, tiled=True)
    result = jnp.transpose(back, (1, 0, 2, 3))
    mine = lax.dynamic_index_in_dim(forces, half, axis=1, keepdims=False)
    theirs = swapped(lax.dynamic_index_in_dim(forces, 1 - half, axis=1, keepdims=False))
    planes = jnp.where(
        half == 0, jnp.stack([mine, theirs], axis=1), jnp.stack([theirs, mine], axis=1)
    )
    return (result, planes.reshape(marker_source.shape))


def solution(mesh):
    split = Mesh(mesh.devices.reshape(8, 2, 8), ("gx", "xh", "zc"))
    gy = ("xh", "zc")
    in_specs = (
        P(None, None, "gx", gy),
        P(None, None, "gx", gy),
        P("gx", gy, None, None, None),
        P("gx", gy, None, None, None),
        P("gx", gy, None, None),
        P("gx", gy, None, None, None, None),
        P(None, "gx", gy, None),
    )
    out_specs = (P(None, None, "gx", gy), P(None, "gx", gy, None))
    return jax.shard_map(
        on_device, mesh=split, in_specs=in_specs, out_specs=out_specs, check_vma=False
    )
```

profile of v0, /device:TPU:0, one launch (start us, length us, event | category | flops | bytes accessed | tf_op | source)
XLA Modules:
  0.0 114.6 jit_solution(13162808013443982199)
XLA Ops:
  0.6 1.3 %copy.9.count_hbm = s32[1,1,3,8]{3,2,1,0:T(4,128)} copy(s32[1,1,3,8]{3,1,2,0:T(1,128)} %param.11) | data formatting | bytes 192 | tf_op args[4]
  1.9 2.4 %shard_map.86 = bf16[16,304,128]{2,1,0:T(8,128)(2,1)} custom-call(s32[1,1,3,8]{3,2,1,0:T(4,128)} %copy.9.count_hbm, f32[2,16,32,128]{3,2,1,0:T(8,128)} %adj_hbm.1, bf16[2,16,32,128]{3,2,1,0:T(8,128)(2,1)} %base_hbm.1, s32[3,8,128]{2,1,0:T(8,128)} %bitcast.15, s32[3,8,128]{2,1,0:T(8,128)} %bitcast.16, f32[3,8,16,128]{3,2,1,0:T(8,128)} %bitcast.13), custom_call_target="tpu_custom_call" | custom-call | tf_op jit(solution)/shard_map/pallas_call | solution.py:52
  4.3 7.1 %all-to-all-start = ((bf16[16,304,128]{2,1,0:T(8,128)(2,1)}), bf16[16,304,128]{2,1,0:T(8,128)(2,1)S(1)}, u32[]{:S(2)}, u32[]{:S(2)}) async-start(bf16[16,304,128]{2,1,0:T(8,128)(2,1)} %shard_map.86), calls=%async_computation | async-start | bytes 2490368 | tf_op jit(solution)/shard_map/all_to_all | solution.py:731
  11.5 3.5 %collective-permute-start = (f32[2,16,128]{2,1,0:T(8,128)S(1)}, f32[2,16,128]{2,1,0:T(8,128)S(1)}, u32[]{:S(2)}, u32[]{:S(2)}) collective-permute-start(f32[2,16,128]{2,1,0:T(8,128)S(1)} %get-tuple-element.81), channel_id=1, source_target_pairs={{0,8},{8,0},{1,9},{9,1},{2,10},{10,2},{3,11},{11,3},{4,12},{12,4},... | collective-permute-start | bytes 49160 | tf_op jit(solution)/shard_map/ppermute | solution.py:88
  15.0 14.0 %collective-permute-done = f32[2,16,128]{2,1,0:T(8,128)S(1)} collective-permute-done((f32[2,16,128]{2,1,0:T(8,128)S(1)}, f32[2,16,128]{2,1,0:T(8,128)S(1)}, u32[]{:S(2)}, u32[]{:S(2)}) %collective-permute-start) | collective-permute-done | bytes 16416 | tf_op jit(solution)/shard_map/ppermute | solution.py:88
  29.0 0.7 all-to-all-done.got_ref
  29.7 0.3 shard_map.88
  30.0 2.0 %collective-permute-start.1 = (f32[2,6,8,256]{3,2,1,0:T(8,128)S(1)}, f32[2,6,8,256]{3,2,1,0:T(8,128)S(1)}, u32[]{:S(2)}, u32[]{:S(2)}) collective-permute-start(f32[2,6,8,256]{3,2,1,0:T(8,128)S(1)} %get-tuple-element.40), channel_id=1, source_target_pairs={{1,2},{3,4},{5,6},{7,0},{2,1},{4,3},{6,5},{0,7},{9,10},{11,12},{13... | collective-permute-start | bytes 294920 | tf_op jit(solution)/shard_map/ppermute | solution.py:83
  32.0 0.1 collective-permute-start.2
  32.1 1.1 shard_map.89.inner_ref
  33.2 2.5 %shard_map.87 = (s32[49,8,128]{2,1,0:T(8,128)S(1)}, f32[49,16,128]{2,1,0:T(8,128)S(1)}, s32[128]{0:T(128)S(1)}) custom-call(bf16[16,304,128]{2,1,0:T(8,128)(2,1)S(1)} %all-to-all-done.got_ref), custom_call_target="tpu_custom_call" | custom-call | tf_op jit(solution)/shard_map/pallas_call | solution.py:52
  35.7 0.0 collective-permute-done.1.far_ref.base_far_ref.thin_far
  35.7 0.0 collective-permute-done.2.near_ref.base_near_ref.thin_near
  35.7 3.4 %shard_map.90 = (f32[2,256,256]{2,1,0:T(8,128)S(1)}, f32[2,2,48,128]{3,2,1,0:T(8,128)S(1)}, f32[2,2,32,128]{3,2,1,0:T(8,128)S(1)}, f32[2,2,32,128]{3,2,1,0:T(8,1...) custom-call(s32[1]{0:T(128)} %bitcast.place_ref, s32[128]{0:T(128)S(1)} %get-tuple-element.39.table_ref, ...), custom_call_target="tpu_custom_call" | custom-call | tf_op jit(solution)/shard_map/pallas_call | solution.py:52
  39.1 2.3 %collective-permute-start.5 = (f32[2,2,32,128]{3,2,1,0:T(8,128)S(1)}, f32[2,2,32,128]{3,2,1,0:T(8,128)S(1)}, u32[]{:S(2)}, u32[]{:S(2)}) collective-permute-start(f32[2,2,32,128]{3,2,1,0:T(8,128)S(1)} %get-tuple-element.49), channel_id=1, source_target_pairs={{1,2},{3,4},{5,6},{7,0},{2,1},{4,3},{6,5},{0,7},{9,10},{11,12},{13... | collective-permute-start | bytes 196616 | tf_op jit(solution)/shard_map/ppermute | solution.py:83
  41.4 0.0 collective-permute-start.6
  41.4 1.5 %collective-permute-start.3 = (f32[2,2,16,128]{3,2,1,0:T(8,128)S(1)}, f32[2,2,16,128]{3,2,1,0:T(8,128)S(1)}, u32[]{:S(2)}, u32[]{:S(2)}) collective-permute-start(f32[2,2,16,128]{3,2,1,0:T(8,128)S(1)} %get-tuple-element.47), channel_id=1, source_target_pairs={{2,4},{3,5},{6,0},{7,1},{4,2},{5,3},{0,6},{1,7},{10,12},{11,13},{1... | collective-permute-start | bytes 98312 | tf_op jit(solution)/shard_map/ppermute | solution.py:83
  43.0 0.2 collective-permute-start.4
  43.2 1.3 %shard_map.91 = (f32[49,128,128]{2,1,0:T(8,128)S(1)}, bf16[49,256,128]{2,1,0:T(8,128)(2,1)S(1)}) custom-call(s32[128]{0:T(128)S(1)} %get-tuple-element.39.table_ref, s32[49,8,128]{2,1,0:T(8,128)S(1)} %get-tuple-element.44.ints_ref, f32[49,16,128]{2,1,0:T(8,128)S(1)} %get-tuple-element.45.weight_ref), custom_call_target="tpu_custom_call" | custom-call | tf_op jit(solution)/shard_map/pallas_call | solution.py:52
  44.4 2.1 %collective-permute-done.3.beyond_far = f32[2,2,16,128]{3,2,1,0:T(8,128)S(1)} collective-permute-done((f32[2,2,16,128]{3,2,1,0:T(8,128)S(1)}, f32[2,2,16,128]{3,2,1,0:T(8,128)S(1)}, u32[]{:S(2)}, u32[]{:S(2)}) %collective-permute-start.3) | collective-permute-done | bytes 32800 | tf_op jit(solution)/shard_map/ppermute | solution.py:83
  46.5 0.3 collective-permute-done.4.beyond_near
  46.9 0.0 collective-permute-done.5.from_far
  46.9 0.0 collective-permute-done.6.from_near
  46.9 3.3 %shard_map.92 = (f32[2,256,256]{2,1,0:T(8,128)S(1)}, bf16[2,2,16,256]{3,2,1,0:T(8,128)(2,1)S(1)}, bf16[2,2,16,256]{3,2,1,0:T(8,128)(2,1)S(1)}, f32[2,2,16,128]{3,2,1,0:T(8,128)}) custom-call(s32[1]{0:T(128)} %bitcast.place_ref, s32[128]{0:T(128)S(1)} %get-tuple-element.39.table_ref, f32[2,2,48,128]{3,2,1,0:T(8,128)S(1)} %get-tuple-element.46.sums_ref, ...), custom_call_target="tpu_custom_call" | custom-call | tf_op jit(solution)/shard_map/pallas_call | solution.py:52
  50.2 0.8 collective-permute-start.7
  51.0 0.0 collective-permute-start.8
  51.0 3.7 %shard_map.93.inner_ref = f32[2,256,256]{2,1,0:T(8,128)S(1)} custom-call(s32[1]{0:T(128)} %bitcast.place_ref, f32[2,256,256]{2,1,0:T(8,128)S(1)} %get-tuple-element.55.mid_ref, f32[2,6,8,256]{3,2,1,0:T(8,128)S(1)} %collective-permute-done.1.far_ref.base_far_ref.thin_far, f32[2,256,256]{2,1,0:T(8,128)S(1)} %get-tuple-element.43.base_ref, ...), custom_call_target="tpu_custom_call" | custom-call | tf_op jit(solution)/shard_map/pallas_call | solution.py:52
  54.7 0.1 collective-permute-done.7.far_ref
  54.8 0.0 collective-permute-done.8.near_ref
  54.8 4.4 %shard_map.94 = (f32[2,256,256]{2,1,0:T(8,128)S(1)}, f32[2,2,48,128]{3,2,1,0:T(8,128)S(1)}, f32[2,2,32,128]{3,2,1,0:T(8,128)S(1)}, f32[2,2,32,128]{3,2,1,0:T(8,1...) custom-call(s32[1]{0:T(128)} %bitcast.place_ref, s32[128]{0:T(128)S(1)} %get-tuple-element.39.table_ref, ...), custom_call_target="tpu_custom_call" | custom-call | tf_op jit(solution)/shard_map/pallas_call | solution.py:52
  59.2 2.2 %collective-permute-start.11 = (f32[2,2,32,128]{3,2,1,0:T(8,128)S(1)}, f32[2,2,32,128]{3,2,1,0:T(8,128)S(1)}, u32[]{:S(2)}, u32[]{:S(2)}) collective-permute-start(f32[2,2,32,128]{3,2,1,0:T(8,128)S(1)} %get-tuple-element.60), channel_id=1, source_target_pairs={{1,2},{3,4},{5,6},{7,0},{2,1},{4,3},{6,5},{0,7},{9,10},{11,12},{13... | collective-permute-start | bytes 196616 | tf_op jit(solution)/shard_map/ppermute | solution.py:83
  61.4 0.0 collective-permute-start.12
  61.5 1.2 %collective-permute-start.9 = (f32[2,2,16,128]{3,2,1,0:T(8,128)S(1)}, f32[2,2,16,128]{3,2,1,0:T(8,128)S(1)}, u32[]{:S(2)}, u32[]{:S(2)}) collective-permute-start(f32[2,2,16,128]{3,2,1,0:T(8,128)S(1)} %get-tuple-element.58), channel_id=1, source_target_pairs={{2,4},{3,5},{6,0},{7,1},{4,2},{5,3},{0,6},{1,7},{10,12},{11,13},{1... | collective-permute-start | bytes 98312 | tf_op jit(solution)/shard_map/ppermute | solution.py:83
  62.6 0.7 collective-permute-start.10
  63.4 3.2 %collective-permute-done.9.beyond_far = f32[2,2,16,128]{3,2,1,0:T(8,128)S(1)} collective-permute-done((f32[2,2,16,128]{3,2,1,0:T(8,128)S(1)}, f32[2,2,16,128]{3,2,1,0:T(8,128)S(1)}, u32[]{:S(2)}, u32[]{:S(2)}) %collective-permute-start.9) | collective-permute-done | bytes 32800 | tf_op jit(solution)/shard_map/ppermute | solution.py:83
  66.6 0.0 collective-permute-done.10.beyond_near
  66.6 0.0 collective-permute-done.12.from_near
  66.6 3.3 %shard_map.95 = (f32[2,256,256]{2,1,0:T(8,128)S(1)}, bf16[2,2,16,256]{3,2,1,0:T(8,128)(2,1)S(1)}, bf16[2,2,16,256]{3,2,1,0:T(8,128)(2,1)S(1)}, f32[2,2,16,128]{3,2,1,0:T(8,128)}) custom-call(s32[1]{0:T(128)} %bitcast.place_ref, s32[128]{0:T(128)S(1)} %get-tuple-element.39.table_ref, f32[2,2,48,128]{3,2,1,0:T(8,128)S(1)} %get-tuple-element.57.sums_ref, ...), custom_call_target="tpu_custom_call" | custom-call | tf_op jit(solution)/shard_map/pallas_call | solution.py:52
  69.9 1.0 collective-permute-start.13
  70.9 0.0 collective-permute-start.14
  70.9 3.7 %shard_map.96.inner_ref = f32[2,256,256]{2,1,0:T(8,128)S(1)} custom-call(s32[1]{0:T(128)} %bitcast.place_ref, f32[2,256,256]{2,1,0:T(8,128)S(1)} %get-tuple-element.64.mid_ref, f32[2,6,8,256]{3,2,1,0:T(8,128)S(1)} %collective-permute-done.1.far_ref.base_far_ref.thin_far, f32[2,256,256]{2,1,0:T(8,128)S(1)} %get-tuple-element.43.base_ref, ...), custom_call_target="tpu_custom_call" | custom-call | tf_op jit(solution)/shard_map/pallas_call | solution.py:52
  74.6 0.0 collective-permute-done.13.far_ref
  74.6 0.0 collective-permute-done.14.near_ref
  74.7 4.4 %shard_map.97 = (f32[2,256,256]{2,1,0:T(8,128)S(1)}, f32[2,2,48,128]{3,2,1,0:T(8,128)S(1)}, f32[2,2,32,128]{3,2,1,0:T(8,128)S(1)}, f32[2,2,32,128]{3,2,1,0:T(8,1...) custom-call(s32[1]{0:T(128)} %bitcast.place_ref, s32[128]{0:T(128)S(1)} %get-tuple-element.39.table_ref, ...), custom_call_target="tpu_custom_call" | custom-call | tf_op jit(solution)/shard_map/pallas_call | solution.py:52
  79.0 2.1 %collective-permute-start.17 = (f32[2,2,32,128]{3,2,1,0:T(8,128)S(1)}, f32[2,2,32,128]{3,2,1,0:T(8,128)S(1)}, u32[]{:S(2)}, u32[]{:S(2)}) collective-permute-start(f32[2,2,32,128]{3,2,1,0:T(8,128)S(1)} %get-tuple-element.69), channel_id=1, source_target_pairs={{1,2},{3,4},{5,6},{7,0},{2,1},{4,3},{6,5},{0,7},{9,10},{11,12},{13... | collective-permute-start | bytes 196616 | tf_op jit(solution)/shard_map/ppermute | solution.py:83
  81.2 0.0 collective-permute-start.18
  81.2 1.3 %collective-permute-start.15 = (f32[2,2,16,128]{3,2,1,0:T(8,128)S(1)}, f32[2,2,16,128]{3,2,1,0:T(8,128)S(1)}, u32[]{:S(2)}, u32[]{:S(2)}) collective-permute-start(f32[2,2,16,128]{3,2,1,0:T(8,128)S(1)} %get-tuple-element.67), channel_id=1, source_target_pairs={{2,4},{3,5},{6,0},{7,1},{4,2},{5,3},{0,6},{1,7},{10,12},{11,13},{1... | collective-permute-start | bytes 98312 | tf_op jit(solution)/shard_map/ppermute | solution.py:83
  82.5 0.6 collective-permute-start.16
  83.1 3.2 %collective-permute-done.15.beyond_far = f32[2,2,16,128]{3,2,1,0:T(8,128)S(1)} collective-permute-done((f32[2,2,16,128]{3,2,1,0:T(8,128)S(1)}, f32[2,2,16,128]{3,2,1,0:T(8,128)S(1)}, u32[]{:S(2)}, u32[]{:S(2)}) %collective-permute-start.15) | collective-permute-done | bytes 32800 | tf_op jit(solution)/shard_map/ppermute | solution.py:83
  86.3 0.1 collective-permute-done.16.beyond_near
  86.4 0.0 collective-permute-done.17.from_far
  86.4 0.0 collective-permute-done.18.from_near
  86.4 3.3 %shard_map.98 = (f32[2,256,256]{2,1,0:T(8,128)S(1)}, bf16[2,2,16,256]{3,2,1,0:T(8,128)(2,1)S(1)}, bf16[2,2,16,256]{3,2,1,0:T(8,128)(2,1)S(1)}, f32[2,2,16,128]{3,2,1,0:T(8,128)S(1)}) custom-call(s32[1]{0:T(128)} %bitcast.place_ref, s32[128]{0:T(128)S(1)} %get-tuple-element.39.table_ref, f32[2,2,48,128]{3,2,1,0:T(8,128)S(1)} %get-tuple-element.66.sums_ref, ...), custom_call_target="tpu_custom_call" | custom-call | tf_op jit(solution)/shard_map/pallas_call | solution.py:52
  89.7 1.0 collective-permute-start.19
  90.7 3.0 %shard_map.99.inner_ref = f32[16,2,32,128]{3,2,1,0:T(8,128)S(1)} custom-call(s32[1]{0:T(128)} %bitcast.place_ref, f32[2,256,256]{2,1,0:T(8,128)S(1)} %get-tuple-element.74.mid_ref), custom_call_target="tpu_custom_call" | custom-call | tf_op jit(solution)/shard_map/pallas_call | solution.py:52
  93.7 0.6 collective-permute-done.19.far_ref
  94.3 0.0 collective-permute-done.20.near_ref
  94.3 1.9 %shard_map.100 = f32[16,2,32,128]{3,2,1,0:T(8,128)} custom-call(s32[1]{0:T(128)} %bitcast.place_ref, bf16[2,2,16,256]{3,2,1,0:T(8,128)(2,1)S(1)} %collective-permute-done.19.far_ref, bf16[2,2,16,256]{3,2,1,0:T(8,128)(2,1)S(1)} %collective-permute-done.20.near_ref, f32[16,2,32,128]{3,2,1,0:T(8,128)S(1)} %shard_map.99.inner_ref), custom_call_target="tpu_custom_call" | custom-call | tf_op jit(solution)/shard_map/pallas_call | solution.py:52
  96.2 6.2 %all-to-all-start.1 = ((f32[16,2,32,128]{3,2,1,0:T(8,128)}), f32[16,2,32,128]{3,2,1,0:T(8,128)S(1)}, u32[]{:S(2)}, u32[]{:S(2)}) async-start(f32[16,2,32,128]{3,2,1,0:T(8,128)} %shard_map.100), calls=%async_computation.1 | async-start | bytes 1048576 | tf_op jit(solution)/shard_map/all_to_all | solution.py:797
  102.5 3.5 %collective-permute-start.21 = (f32[2,16,128]{2,1,0:T(8,128)S(1)}, f32[2,16,128]{2,1,0:T(8,128)S(1)}, u32[]{:S(2)}, u32[]{:S(2)}) collective-permute-start(f32[2,16,128]{2,1,0:T(8,128)S(1)} %get-tuple-element.79), channel_id=1, source_target_pairs={{0,8},{8,0},{1,9},{9,1},{2,10},{10,2},{3,11},{11,3},{4,12},{12,4},... | collective-permute-start | bytes 49160 | tf_op jit(solution)/shard_map/ppermute | solution.py:88
  106.0 6.3 %collective-permute-done.21 = f32[2,16,128]{2,1,0:T(8,128)S(1)} collective-permute-done((f32[2,16,128]{2,1,0:T(8,128)S(1)}, f32[2,16,128]{2,1,0:T(8,128)S(1)}, u32[]{:S(2)}, u32[]{:S(2)}) %collective-permute-start.21) | collective-permute-done | bytes 16416 | tf_op jit(solution)/shard_map/ppermute | solution.py:88
  112.2 0.6 maximum_select_fusion.1
  112.9 0.9 all-to-all-done.1
  113.7 0.8 copy.10
  (10 shorter events, 0.1 us)
Async XLA Ops:
  0.6 10.8 %copy-start = (f32[2,2,4,512]{3,2,1,0:T(4,128)S(1)}, f32[2,2,4,512]{3,2,1,0:T(4,128)}, u32[]{:S(2)}) copy-start(f32[2,2,4,512]{3,2,1,0:T(4,128)} %param.13) | copy-start | bytes 98308
  4.3 25.4 %all-to-all-start = ((bf16[16,304,128]{2,1,0:T(8,128)(2,1)}), bf16[16,304,128]{2,1,0:T(8,128)(2,1)S(1)}, u32[]{:S(2)}, u32[]{:S(2)}) async-start(bf16[16,304,128]{2,1,0:T(8,128)(2,1)} %shard_map.86), calls=%async_computation | async-start | bytes 2490368 | tf_op jit(solution)/shard_map/all_to_all | solution.py:731
  11.5 17.5 %collective-permute-start = (f32[2,16,128]{2,1,0:T(8,128)S(1)}, f32[2,16,128]{2,1,0:T(8,128)S(1)}, u32[]{:S(2)}, u32[]{:S(2)}) collective-permute-start(f32[2,16,128]{2,1,0:T(8,128)S(1)} %get-tuple-element.81), channel_id=1, source_target_pairs={{0,8},{8,0},{1,9},{9,1},{2,10},{10,2},{3,11},{11,3},{4,12},{12,4},... | collective-permute-start | bytes 49160 | tf_op jit(solution)/shard_map/ppermute | solution.py:88
  30.0 5.7 %collective-permute-start.1 = (f32[2,6,8,256]{3,2,1,0:T(8,128)S(1)}, f32[2,6,8,256]{3,2,1,0:T(8,128)S(1)}, u32[]{:S(2)}, u32[]{:S(2)}) collective-permute-start(f32[2,6,8,256]{3,2,1,0:T(8,128)S(1)} %get-tuple-element.40), channel_id=1, source_target_pairs={{1,2},{3,4},{5,6},{7,0},{2,1},{4,3},{6,5},{0,7},{9,10},{11,12},{13... | collective-permute-start | bytes 294920 | tf_op jit(solution)/shard_map/ppermute | solution.py:83
  32.0 3.7 %collective-permute-start.2 = (f32[2,6,8,256]{3,2,1,0:T(8,128)S(1)}, f32[2,6,8,256]{3,2,1,0:T(8,128)S(1)}, u32[]{:S(2)}, u32[]{:S(2)}) collective-permute-start(f32[2,6,8,256]{3,2,1,0:T(8,128)S(1)} %get-tuple-element.42), channel_id=1, source_target_pairs={{0,1},{2,3},{4,5},{6,7},{1,0},{3,2},{5,4},{7,6},{8,9},{10,11},{12,... | collective-permute-start | bytes 294920 | tf_op jit(solution)/shard_map/ppermute | solution.py:83
  39.1 7.8 %collective-permute-start.5 = (f32[2,2,32,128]{3,2,1,0:T(8,128)S(1)}, f32[2,2,32,128]{3,2,1,0:T(8,128)S(1)}, u32[]{:S(2)}, u32[]{:S(2)}) collective-permute-start(f32[2,2,32,128]{3,2,1,0:T(8,128)S(1)} %get-tuple-element.49), channel_id=1, source_target_pairs={{1,2},{3,4},{5,6},{7,0},{2,1},{4,3},{6,5},{0,7},{9,10},{11,12},{13... | collective-permute-start | bytes 196616 | tf_op jit(solution)/shard_map/ppermute | solution.py:83
  41.4 5.5 %collective-permute-start.6 = (f32[2,2,32,128]{3,2,1,0:T(8,128)S(1)}, f32[2,2,32,128]{3,2,1,0:T(8,128)S(1)}, u32[]{:S(2)}, u32[]{:S(2)}) collective-permute-start(f32[2,2,32,128]{3,2,1,0:T(8,128)S(1)} %get-tuple-element.50), channel_id=1, source_target_pairs={{0,1},{2,3},{4,5},{6,7},{1,0},{3,2},{5,4},{7,6},{8,9},{10,11},{12,... | collective-permute-start | bytes 196616 | tf_op jit(solution)/shard_map/ppermute | solution.py:83
  41.4 5.1 %collective-permute-start.3 = (f32[2,2,16,128]{3,2,1,0:T(8,128)S(1)}, f32[2,2,16,128]{3,2,1,0:T(8,128)S(1)}, u32[]{:S(2)}, u32[]{:S(2)}) collective-permute-start(f32[2,2,16,128]{3,2,1,0:T(8,128)S(1)} %get-tuple-element.47), channel_id=1, source_target_pairs={{2,4},{3,5},{6,0},{7,1},{4,2},{5,3},{0,6},{1,7},{10,12},{11,13},{1... | collective-permute-start | bytes 98312 | tf_op jit(solution)/shard_map/ppermute | solution.py:83
  43.0 3.9 %collective-permute-start.4 = (f32[2,2,16,128]{3,2,1,0:T(8,128)S(1)}, f32[2,2,16,128]{3,2,1,0:T(8,128)S(1)}, u32[]{:S(2)}, u32[]{:S(2)}) collective-permute-start(f32[2,2,16,128]{3,2,1,0:T(8,128)S(1)} %get-tuple-element.48), channel_id=1, source_target_pairs={{0,2},{1,3},{4,6},{5,7},{2,0},{3,1},{6,4},{7,5},{8,10},{9,11},{12,... | collective-permute-start | bytes 98312 | tf_op jit(solution)/shard_map/ppermute | solution.py:83
  50.2 4.6 %collective-permute-start.7 = (bf16[2,2,16,256]{3,2,1,0:T(8,128)(2,1)S(1)}, bf16[2,2,16,256]{3,2,1,0:T(8,128)(2,1)S(1)}, u32[]{:S(2)}, u32[]{:S(2)}) collective-permute-start(bf16[2,2,16,256]{3,2,1,0:T(8,128)(2,1)S(1)} %get-tuple-element.54), channel_id=1, source_target_pairs={{1,2},{3,4},{5,6},{7,0},{2,1},{4,3},{6,5},{0,7},{9,10},{11,12},{13... | collective-permute-start | bytes 98312 | tf_op jit(solution)/shard_map/ppermute | solution.py:83
  51.0 3.9 %collective-permute-start.8 = (bf16[2,2,16,256]{3,2,1,0:T(8,128)(2,1)S(1)}, bf16[2,2,16,256]{3,2,1,0:T(8,128)(2,1)S(1)}, u32[]{:S(2)}, u32[]{:S(2)}) collective-permute-start(bf16[2,2,16,256]{3,2,1,0:T(8,128)(2,1)S(1)} %get-tuple-element.56), channel_id=1, source_target_pairs={{0,1},{2,3},{4,5},{6,7},{1,0},{3,2},{5,4},{7,6},{8,9},{10,11},{12,... | collective-permute-start | bytes 98312 | tf_op jit(solution)/shard_map/ppermute | solution.py:83
  59.2 7.4 %collective-permute-start.11 = (f32[2,2,32,128]{3,2,1,0:T(8,128)S(1)}, f32[2,2,32,128]{3,2,1,0:T(8,128)S(1)}, u32[]{:S(2)}, u32[]{:S(2)}) collective-permute-start(f32[2,2,32,128]{3,2,1,0:T(8,128)S(1)} %get-tuple-element.60), channel_id=1, source_target_pairs={{1,2},{3,4},{5,6},{7,0},{2,1},{4,3},{6,5},{0,7},{9,10},{11,12},{13... | collective-permute-start | bytes 196616 | tf_op jit(solution)/shard_map/ppermute | solution.py:83
  61.4 5.1 %collective-permute-start.12 = (f32[2,2,32,128]{3,2,1,0:T(8,128)S(1)}, f32[2,2,32,128]{3,2,1,0:T(8,128)S(1)}, u32[]{:S(2)}, u32[]{:S(2)}) collective-permute-start(f32[2,2,32,128]{3,2,1,0:T(8,128)S(1)} %get-tuple-element.61), channel_id=1, source_target_pairs={{0,1},{2,3},{4,5},{6,7},{1,0},{3,2},{5,4},{7,6},{8,9},{10,11},{12,... | collective-permute-start | bytes 196616 | tf_op jit(solution)/shard_map/ppermute | solution.py:83
  61.5 5.1 %collective-permute-start.9 = (f32[2,2,16,128]{3,2,1,0:T(8,128)S(1)}, f32[2,2,16,128]{3,2,1,0:T(8,128)S(1)}, u32[]{:S(2)}, u32[]{:S(2)}) collective-permute-start(f32[2,2,16,128]{3,2,1,0:T(8,128)S(1)} %get-tuple-element.58), channel_id=1, source_target_pairs={{2,4},{3,5},{6,0},{7,1},{4,2},{5,3},{0,6},{1,7},{10,12},{11,13},{1... | collective-permute-start | bytes 98312 | tf_op jit(solution)/shard_map/ppermute | solution.py:83
  62.6 3.9 %collective-permute-start.10 = (f32[2,2,16,128]{3,2,1,0:T(8,128)S(1)}, f32[2,2,16,128]{3,2,1,0:T(8,128)S(1)}, u32[]{:S(2)}, u32[]{:S(2)}) collective-permute-start(f32[2,2,16,128]{3,2,1,0:T(8,128)S(1)} %get-tuple-element.59), channel_id=1, source_target_pairs={{0,2},{1,3},{4,6},{5,7},{2,0},{3,1},{6,4},{7,5},{8,10},{9,11},{12,... | collective-permute-start | bytes 98312 | tf_op jit(solution)/shard_map/ppermute | solution.py:83
  69.9 4.7 %collective-permute-start.13 = (bf16[2,2,16,256]{3,2,1,0:T(8,128)(2,1)S(1)}, bf16[2,2,16,256]{3,2,1,0:T(8,128)(2,1)S(1)}, u32[]{:S(2)}, u32[]{:S(2)}) collective-permute-start(bf16[2,2,16,256]{3,2,1,0:T(8,128)(2,1)S(1)} %get-tuple-element.63), channel_id=1, source_target_pairs={{1,2},{3,4},{5,6},{7,0},{2,1},{4,3},{6,5},{0,7},{9,10},{11,12},{13... | collective-permute-start | bytes 98312 | tf_op jit(solution)/shard_map/ppermute | solution.py:83
  70.9 3.7 %collective-permute-start.14 = (bf16[2,2,16,256]{3,2,1,0:T(8,128)(2,1)S(1)}, bf16[2,2,16,256]{3,2,1,0:T(8,128)(2,1)S(1)}, u32[]{:S(2)}, u32[]{:S(2)}) collective-permute-start(bf16[2,2,16,256]{3,2,1,0:T(8,128)(2,1)S(1)} %get-tuple-element.65), channel_id=1, source_target_pairs={{0,1},{2,3},{4,5},{6,7},{1,0},{3,2},{5,4},{7,6},{8,9},{10,11},{12,... | collective-permute-start | bytes 98312 | tf_op jit(solution)/shard_map/ppermute | solution.py:83
  79.0 7.4 %collective-permute-start.17 = (f32[2,2,32,128]{3,2,1,0:T(8,128)S(1)}, f32[2,2,32,128]{3,2,1,0:T(8,128)S(1)}, u32[]{:S(2)}, u32[]{:S(2)}) collective-permute-start(f32[2,2,32,128]{3,2,1,0:T(8,128)S(1)} %get-tuple-element.69), channel_id=1, source_target_pairs={{1,2},{3,4},{5,6},{7,0},{2,1},{4,3},{6,5},{0,7},{9,10},{11,12},{13... | collective-permute-start | bytes 196616 | tf_op jit(solution)/shard_map/ppermute | solution.py:83
  81.2 5.2 %collective-permute-start.18 = (f32[2,2,32,128]{3,2,1,0:T(8,128)S(1)}, f32[2,2,32,128]{3,2,1,0:T(8,128)S(1)}, u32[]{:S(2)}, u32[]{:S(2)}) collective-permute-start(f32[2,2,32,128]{3,2,1,0:T(8,128)S(1)} %get-tuple-element.70), channel_id=1, source_target_pairs={{0,1},{2,3},{4,5},{6,7},{1,0},{3,2},{5,4},{7,6},{8,9},{10,11},{12,... | collective-permute-start | bytes 196616 | tf_op jit(solution)/shard_map/ppermute | solution.py:83
  81.2 5.1 %collective-permute-start.15 = (f32[2,2,16,128]{3,2,1,0:T(8,128)S(1)}, f32[2,2,16,128]{3,2,1,0:T(8,128)S(1)}, u32[]{:S(2)}, u32[]{:S(2)}) collective-permute-start(f32[2,2,16,128]{3,2,1,0:T(8,128)S(1)} %get-tuple-element.67), channel_id=1, source_target_pairs={{2,4},{3,5},{6,0},{7,1},{4,2},{5,3},{0,6},{1,7},{10,12},{11,13},{1... | collective-permute-start | bytes 98312 | tf_op jit(solution)/shard_map/ppermute | solution.py:83
  82.5 3.9 %collective-permute-start.16 = (f32[2,2,16,128]{3,2,1,0:T(8,128)S(1)}, f32[2,2,16,128]{3,2,1,0:T(8,128)S(1)}, u32[]{:S(2)}, u32[]{:S(2)}) collective-permute-start(f32[2,2,16,128]{3,2,1,0:T(8,128)S(1)} %get-tuple-element.68), channel_id=1, source_target_pairs={{0,2},{1,3},{4,6},{5,7},{2,0},{3,1},{6,4},{7,5},{8,10},{9,11},{12,... | collective-permute-start | bytes 98312 | tf_op jit(solution)/shard_map/ppermute | solution.py:83
  89.7 4.6 %collective-permute-start.19 = (bf16[2,2,16,256]{3,2,1,0:T(8,128)(2,1)S(1)}, bf16[2,2,16,256]{3,2,1,0:T(8,128)(2,1)S(1)}, u32[]{:S(2)}, u32[]{:S(2)}) collective-permute-start(bf16[2,2,16,256]{3,2,1,0:T(8,128)(2,1)S(1)} %get-tuple-element.72), channel_id=1, source_target_pairs={{1,2},{3,4},{5,6},{7,0},{2,1},{4,3},{6,5},{0,7},{9,10},{11,12},{13... | collective-permute-start | bytes 98312 | tf_op jit(solution)/shard_map/ppermute | solution.py:83
  90.7 3.6 %collective-permute-start.20 = (bf16[2,2,16,256]{3,2,1,0:T(8,128)(2,1)S(1)}, bf16[2,2,16,256]{3,2,1,0:T(8,128)(2,1)S(1)}, u32[]{:S(2)}, u32[]{:S(2)}) collective-permute-start(bf16[2,2,16,256]{3,2,1,0:T(8,128)(2,1)S(1)} %get-tuple-element.73), channel_id=1, source_target_pairs={{0,1},{2,3},{4,5},{6,7},{1,0},{3,2},{5,4},{7,6},{8,9},{10,11},{12,... | collective-permute-start | bytes 98312 | tf_op jit(solution)/shard_map/ppermute | solution.py:83
  96.2 17.5 %all-to-all-start.1 = ((f32[16,2,32,128]{3,2,1,0:T(8,128)}), f32[16,2,32,128]{3,2,1,0:T(8,128)S(1)}, u32[]{:S(2)}, u32[]{:S(2)}) async-start(f32[16,2,32,128]{3,2,1,0:T(8,128)} %shard_map.100), calls=%async_computation.1 | async-start | bytes 1048576 | tf_op jit(solution)/shard_map/all_to_all | solution.py:797
  102.5 9.8 %collective-permute-start.21 = (f32[2,16,128]{2,1,0:T(8,128)S(1)}, f32[2,16,128]{2,1,0:T(8,128)S(1)}, u32[]{:S(2)}, u32[]{:S(2)}) collective-permute-start(f32[2,16,128]{2,1,0:T(8,128)S(1)} %get-tuple-element.79), channel_id=1, source_target_pairs={{0,8},{8,0},{1,9},{9,1},{2,10},{10,2},{3,11},{11,3},{4,12},{12,4},... | collective-permute-start | bytes 49160 | tf_op jit(solution)/shard_map/ppermute | solution.py:88
where the time goes:
time: 115 us
  Pallas kernels  42 us (37%)
  starting transfers between devices  37.5 us (33%)
  waiting for transfers between devices  31.5 us (27%)
  local copies, waits for them, and re-layouts  2.16 us (2%)
    pallas_call x15, Pallas kernels, call(): pl.pallas_call(body, out_shape=outs, in_specs=[spaces.get(n, VMEM) for n...  42 us
    ppermute x2, waiting for transfers between devices, swapped(): return lax.ppermute(value, 'xh', [(0, 1), (1, 0)])  20.3 us
    ppermute x20, starting transfers between devices, exchanged(): results.append(lax.ppermute(value, 'zc', pairs))  17.1 us
    ppermute x20, waiting for transfers between devices, exchanged(): results.append(lax.ppermute(value, 'zc', pairs))  9.69 us
    all_to_all x1, starting transfers between devices, on_device(): got = lax.all_to_all(packed, whole, split_axis=0, concat_axis=0, tiled=True)  7.13 us
    ppermute x2, starting transfers between devices, swapped(): return lax.ppermute(value, 'xh', [(0, 1), (1, 0)])  6.99 us
    all_to_all x1, starting transfers between devices, on_device(): back = lax.all_to_all(done, whole, split_axis=0, concat_axis=0, tiled=True)  6.18 us
  transfers between devices with their start and end apart: 24, of which 11 were waited for; matrix products, arithmetic and copies ran while one was open for 1% of the time, Pallas kernels for 13%

commit v1 on v0

--- a/solution.py
+++ b/solution.py
@@ -486,13 +486,6 @@
             pick_ref[2 * a + side, at : at + ROWS, :] = both[a * ROWS : (a + 1) * ROWS]
 
 
-def first_inner_kernel(mid_ref, base_ref, moved_ref):
-    w = [mid_ref[c] for c in range(2)]
-    out = transported(w, [base_ref[c] for c in range(2)])
-    for c in range(2):
-        moved_ref[c] = out[c]
-
-
 def inner_kernel(place_ref, mid_ref, base_far_ref, base_ref, base_near_ref, moved_ref):
     place = place_ref[0]
     extra = RIM - THIN
@@ -512,47 +505,63 @@
             moved_ref[c, side * COLS : (side + 1) * COLS, :] = out[c][at : at + COLS]
 
 
+def first_moved(place, far_ref, mid_ref, near_ref, base_ref):
+    w, base = (
+        [widened(ref, c, *thin_rims(place, far_ref, near_ref, at + c)) for c in range(2)]
+        for ref, at in ((mid_ref, 0), (base_ref, 2))
+    )
+    length = COLS + 2 * THIN
+    return [
+        [x[side * length + THIN : side * length + THIN + COLS] for side in range(2)]
+        for x in transported(w, base)
+    ]
+
+
+def later_moved(place, far_ref, near_ref, base_far_ref, base_ref, base_near_ref, inner_ref):
+    blank = jnp.zeros((RIM - THIN, NROW), F32)
+    base = []
+    for c in range(2):
+        lows, highs = thin_rims(place, base_far_ref, base_near_ref, 2 + c)
+        lows = [jnp.concatenate([blank, x], axis=0) for x in lows]
+        highs = [jnp.concatenate([x, blank], axis=0) for x in highs]
+        base.append(strips(lows, highs, base_ref, c))
+    out = transported(projected(rim_strips(place, far_ref, near_ref), masked(place)), base)
+    moved = []
+    for c in range(2):
+        tiles = []
+        for side in range(2):
+            low, high = outer_columns(out[c], side)
+            at = side * COLS
+            tiles.append(
+                jnp.concatenate(
+                    [
+                        inner_ref[c, at : at + RIM, :] + low,
+                        inner_ref[c, at + RIM : at + COLS - RIM, :],
+                        inner_ref[c, at + COLS - RIM : at + COLS, :] + high,
+                    ],
+                    axis=0,
+                )
+            )
+        moved.append(tiles)
+    return moved
+
+
 def outer_kernel(
-    first, place_ref, table_ref, far_ref, mid_ref, near_ref, base_far_ref, base_ref,
-    base_near_ref, ints_ref, weight_ref, inner_ref, moved_ref, own_ref, part_far, part_near,
+    first, place_ref, table_ref, far_ref, near_ref, base_far_ref, base_ref, base_near_ref,
+    ints_ref, weight_ref, inner_ref, moved_ref, own_ref, part_far, part_near,
     next_far, next_near, pick_ref, sum_ref, *got_refs,
 ):
     place = place_ref[0]
-    blank = jnp.zeros((RIM - THIN, NROW), F32)
-
-    def thin_strips(far, mid, near, c, at):
-        lows, highs = thin_rims(place, far, near, at + c)
-        return strips(
-            [jnp.concatenate([blank, x], axis=0) for x in lows],
-            [jnp.concatenate([x, blank], axis=0) for x in highs],
-            mid,
-            c,
-        )
-
-    base = [thin_strips(base_far_ref, base_ref, base_near_ref, c, 2) for c in range(2)]
     if first:
-        w = [thin_strips(far_ref, mid_ref, near_ref, c, 0) for c in range(2)]
+        moved = first_moved(place, far_ref, inner_ref, near_ref, base_ref)
     else:
-        w = projected(rim_strips(place, far_ref, near_ref), masked(place))
-    out = transported(w, base)
-    spot = lax.broadcasted_iota(I32, (RIM, NROW), 0)
-    for c in range(2):
-        for side in range(2):
-            low, high = outer_columns(out[c], side)
-            at = side * COLS
-            old_low = inner_ref[c, at : at + RIM, :]
-            old_high = inner_ref[c, at + COLS - RIM : at + COLS, :]
-            if first:
-                low = jnp.where(spot == 0, low, old_low)
-                high = jnp.where(spot == RIM - 1, high, old_high)
-            else:
-                low = old_low + low
-                high = old_high + high
-            moved = jnp.concatenate(
-                [low, inner_ref[c, at + RIM : at + COLS - RIM, :], high], axis=0
-            )
-            moved_ref[c, at : at + COLS, :] = moved
-            pick(moved.T, c, side, pick_ref)
+        moved = later_moved(
+            place, far_ref, near_ref, base_far_ref, base_ref, base_near_ref, inner_ref
+        )
+    for c in range(2):
+        for side in range(2):
+            moved_ref[c, side * COLS : (side + 1) * COLS, :] = moved[c][side]
+            pick(moved[c][side].T, c, side, pick_ref)
     interpolate(table_ref, ints_ref, weight_ref, pick_ref, got_refs, sum_ref)
     sums = sum_ref[...].T
     sums = sums[:KEPT] + sums[KEPT:]
@@ -753,7 +762,7 @@
     row_tables = col_tables = None
     for substep in range(SUBSTEPS):
         if substep == 0:
-            inner = call(first_inner_kernel, field, (current, base))
+            inner = current
         else:
             inner = call(
                 inner_kernel,
@@ -764,7 +773,7 @@
         moved, sums, part_far, part_near, next_far, next_near = call(
             functools.partial(outer_kernel, substep == 0),
             (field, shape(2, 2, 48, COLS), part, part, beyond, beyond),
-            (place, table, far, current, near, base_far, base, base_near, ints, weights, inner),
+            (place, table, far, near, base_far, base, base_near, ints, weights, inner),
             scratch=OUTER_SCRATCH,
             spaces={0: SMEM, 1: SMEM},
         )

time: 115 us -> 115 us (level)
    pallas_call x15 -> x14, Pallas kernels: 42 us -> 41.5 us  [call(): pl.pallas_call(body, out_shape=outs, in_specs=[spaces.get(n, VMEM) for n...]
  transfers between devices with their start and end apart: 24 -> 24, of which waited for: 11 -> 12; matrix products, arithmetic and copies ran while one was open for 1% -> 1% of each run, Pallas kernels for 13% -> 12%
where the time goes in v1:
time: 115 us
  Pallas kernels  41.5 us (36%)
  starting transfers between devices  37.9 us (33%)
  waiting for transfers between devices  31.7 us (28%)
  local copies, waits for them, and re-layouts  2.16 us (2%)
    pallas_call x14, Pallas kernels, call(): pl.pallas_call(body, out_shape=outs, in_specs=[spaces.get(n, VMEM) for n...  41.5 us
    ppermute x2, waiting for transfers between devices, swapped(): return lax.ppermute(value, 'xh', [(0, 1), (1, 0)])  20.3 us
    ppermute x20, starting transfers between devices, exchanged(): results.append(lax.ppermute(value, 'zc', pairs))  17.5 us
    ppermute x20, waiting for transfers between devices, exchanged(): results.append(lax.ppermute(value, 'zc', pairs))  9.87 us
    all_to_all x1, starting transfers between devices, on_device(): got = lax.all_to_all(packed, whole, split_axis=0, concat_axis=0, tiled=True)  7.13 us
    ppermute x2, starting transfers between devices, swapped(): return lax.ppermute(value, 'xh', [(0, 1), (1, 0)])  6.99 us
    all_to_all x1, starting transfers between devices, on_device(): back = lax.all_to_all(done, whole, split_axis=0, concat_axis=0, tiled=True)  6.24 us
  transfers between devices with their start and end apart: 24, of which 12 were waited for; matrix products, arithmetic and copies ran while one was open for 1% of the time, Pallas kernels for 12%

profile of v1, /device:TPU:0, one launch (start us, length us, event | category | flops | bytes accessed | tf_op | source)
XLA Modules:
  0.0 114.7 jit_solution(2495863956014976535)
XLA Ops:
  0.6 1.3 %copy.9.count_hbm = s32[1,1,3,8]{3,2,1,0:T(4,128)} copy(s32[1,1,3,8]{3,1,2,0:T(1,128)} %param.11) | data formatting | bytes 192 | tf_op args[4]
  1.9 2.4 %shard_map.86 = bf16[16,304,128]{2,1,0:T(8,128)(2,1)} custom-call(s32[1,1,3,8]{3,2,1,0:T(4,128)} %copy.9.count_hbm, f32[2,16,32,128]{3,2,1,0:T(8,128)} %adj_hbm.1, bf16[2,16,32,128]{3,2,1,0:T(8,128)(2,1)} %base_hbm.1, s32[3,8,128]{2,1,0:T(8,128)} %bitcast.15, s32[3,8,128]{2,1,0:T(8,128)} %bitcast.16, f32[3,8,16,128]{3,2,1,0:T(8,128)} %bitcast.13), custom_call_target="tpu_custom_call" | custom-call | tf_op jit(solution)/shard_map/pallas_call | solution.py:52
  4.3 7.1 %all-to-all-start = ((bf16[16,304,128]{2,1,0:T(8,128)(2,1)}), bf16[16,304,128]{2,1,0:T(8,128)(2,1)S(1)}, u32[]{:S(2)}, u32[]{:S(2)}) async-start(bf16[16,304,128]{2,1,0:T(8,128)(2,1)} %shard_map.86), calls=%async_computation | async-start | bytes 2490368 | tf_op jit(solution)/shard_map/all_to_all | solution.py:740
  11.5 3.5 %collective-permute-start = (f32[2,16,128]{2,1,0:T(8,128)S(1)}, f32[2,16,128]{2,1,0:T(8,128)S(1)}, u32[]{:S(2)}, u32[]{:S(2)}) collective-permute-start(f32[2,16,128]{2,1,0:T(8,128)S(1)} %get-tuple-element.81), channel_id=1, source_target_pairs={{0,8},{8,0},{1,9},{9,1},{2,10},{10,2},{3,11},{11,3},{4,12},{12,4},... | collective-permute-start | bytes 49160 | tf_op jit(solution)/shard_map/ppermute | solution.py:88
  15.0 14.0 %collective-permute-done = f32[2,16,128]{2,1,0:T(8,128)S(1)} collective-permute-done((f32[2,16,128]{2,1,0:T(8,128)S(1)}, f32[2,16,128]{2,1,0:T(8,128)S(1)}, u32[]{:S(2)}, u32[]{:S(2)}) %collective-permute-start) | collective-permute-done | bytes 16416 | tf_op jit(solution)/shard_map/ppermute | solution.py:88
  29.0 0.7 all-to-all-done.got_ref
  29.7 0.3 shard_map.88
  30.0 2.0 %collective-permute-start.1 = (f32[2,6,8,256]{3,2,1,0:T(8,128)S(1)}, f32[2,6,8,256]{3,2,1,0:T(8,128)S(1)}, u32[]{:S(2)}, u32[]{:S(2)}) collective-permute-start(f32[2,6,8,256]{3,2,1,0:T(8,128)S(1)} %get-tuple-element.40), channel_id=1, source_target_pairs={{1,2},{3,4},{5,6},{7,0},{2,1},{4,3},{6,5},{0,7},{9,10},{11,12},{13... | collective-permute-start | bytes 294920 | tf_op jit(solution)/shard_map/ppermute | solution.py:83
  32.0 0.1 collective-permute-start.2
  32.1 2.5 %shard_map.87 = (s32[49,8,128]{2,1,0:T(8,128)S(1)}, f32[49,16,128]{2,1,0:T(8,128)S(1)}, s32[128]{0:T(128)S(1)}) custom-call(bf16[16,304,128]{2,1,0:T(8,128)(2,1)S(1)} %all-to-all-done.got_ref), custom_call_target="tpu_custom_call" | custom-call | tf_op jit(solution)/shard_map/pallas_call | solution.py:52
  34.6 0.7 collective-permute-done.1.far_ref.base_far_ref.thin_far
  35.3 0.0 collective-permute-done.2.near_ref.base_near_ref.thin_near
  35.3 4.2 %shard_map.89 = (f32[2,256,256]{2,1,0:T(8,128)S(1)}, f32[2,2,48,128]{3,2,1,0:T(8,128)S(1)}, f32[2,2,32,128]{3,2,1,0:T(8,128)S(1)}, f32[2,2,32,128]{3,2,1,0:T(8,1...) custom-call(s32[1]{0:T(128)} %bitcast.place_ref, s32[128]{0:T(128)S(1)} %get-tuple-element.39.table_ref, ...), custom_call_target="tpu_custom_call" | custom-call | tf_op jit(solution)/shard_map/pallas_call | solution.py:52
  39.5 2.0 %collective-permute-start.5 = (f32[2,2,32,128]{3,2,1,0:T(8,128)S(1)}, f32[2,2,32,128]{3,2,1,0:T(8,128)S(1)}, u32[]{:S(2)}, u32[]{:S(2)}) collective-permute-start(f32[2,2,32,128]{3,2,1,0:T(8,128)S(1)} %get-tuple-element.49), channel_id=1, source_target_pairs={{1,2},{3,4},{5,6},{7,0},{2,1},{4,3},{6,5},{0,7},{9,10},{11,12},{13... | collective-permute-start | bytes 196616 | tf_op jit(solution)/shard_map/ppermute | solution.py:83
  41.5 0.0 collective-permute-start.6
  41.5 1.4 %collective-permute-start.3 = (f32[2,2,16,128]{3,2,1,0:T(8,128)S(1)}, f32[2,2,16,128]{3,2,1,0:T(8,128)S(1)}, u32[]{:S(2)}, u32[]{:S(2)}) collective-permute-start(f32[2,2,16,128]{3,2,1,0:T(8,128)S(1)} %get-tuple-element.47), channel_id=1, source_target_pairs={{2,4},{3,5},{6,0},{7,1},{4,2},{5,3},{0,6},{1,7},{10,12},{11,13},{1... | collective-permute-start | bytes 98312 | tf_op jit(solution)/shard_map/ppermute | solution.py:83
  43.0 1.0 collective-permute-start.4
  44.0 1.3 %shard_map.90 = (f32[49,128,128]{2,1,0:T(8,128)S(1)}, bf16[49,256,128]{2,1,0:T(8,128)(2,1)S(1)}) custom-call(s32[128]{0:T(128)S(1)} %get-tuple-element.39.table_ref, s32[49,8,128]{2,1,0:T(8,128)S(1)} %get-tuple-element.43.ints_ref, f32[49,16,128]{2,1,0:T(8,128)S(1)} %get-tuple-element.44.weight_ref), custom_call_target="tpu_custom_call" | custom-call | tf_op jit(solution)/shard_map/pallas_call | solution.py:52
  45.2 1.4 %collective-permute-done.3.beyond_far = f32[2,2,16,128]{3,2,1,0:T(8,128)S(1)} collective-permute-done((f32[2,2,16,128]{3,2,1,0:T(8,128)S(1)}, f32[2,2,16,128]{3,2,1,0:T(8,128)S(1)}, u32[]{:S(2)}, u32[]{:S(2)}) %collective-permute-start.3) | collective-permute-done | bytes 32800 | tf_op jit(solution)/shard_map/ppermute | solution.py:83
  46.6 0.2 collective-permute-done.4.beyond_near
  46.9 0.0 collective-permute-done.5.from_far
  46.9 0.0 collective-permute-done.6.from_near
  46.9 3.3 %shard_map.91 = (f32[2,256,256]{2,1,0:T(8,128)S(1)}, bf16[2,2,16,256]{3,2,1,0:T(8,128)(2,1)S(1)}, bf16[2,2,16,256]{3,2,1,0:T(8,128)(2,1)S(1)}, f32[2,2,16,128]{3,2,1,0:T(8,128)}) custom-call(s32[1]{0:T(128)} %bitcast.place_ref, s32[128]{0:T(128)S(1)} %get-tuple-element.39.table_ref, f32[2,2,48,128]{3,2,1,0:T(8,128)S(1)} %get-tuple-element.46.sums_ref, ...), custom_call_target="tpu_custom_call" | custom-call | tf_op jit(solution)/shard_map/pallas_call | solution.py:52
  50.1 0.9 collective-permute-start.7
  51.0 0.3 collective-permute-start.8
  51.4 3.7 %shard_map.92.inner_ref = f32[2,256,256]{2,1,0:T(8,128)S(1)} custom-call(s32[1]{0:T(128)} %bitcast.place_ref, f32[2,256,256]{2,1,0:T(8,128)S(1)} %get-tuple-element.56.mid_ref, f32[2,6,8,256]{3,2,1,0:T(8,128)S(1)} %collective-permute-done.1.far_ref.base_far_ref.thin_far, f32[2,256,256]{2,1,0:T(8,128)S(1)} %get-tuple-element.42.base_ref, ...), custom_call_target="tpu_custom_call" | custom-call | tf_op jit(solution)/shard_map/pallas_call | solution.py:52
  55.1 0.0 collective-permute-done.7.far_ref
  55.1 0.0 collective-permute-done.8.near_ref
  55.1 4.4 %shard_map.93 = (f32[2,256,256]{2,1,0:T(8,128)S(1)}, f32[2,2,48,128]{3,2,1,0:T(8,128)S(1)}, f32[2,2,32,128]{3,2,1,0:T(8,128)S(1)}, f32[2,2,32,128]{3,2,1,0:T(8,1...) custom-call(s32[1]{0:T(128)} %bitcast.place_ref, s32[128]{0:T(128)S(1)} %get-tuple-element.39.table_ref, ...), custom_call_target="tpu_custom_call" | custom-call | tf_op jit(solution)/shard_map/pallas_call | solution.py:52
  59.5 1.9 %collective-permute-start.11 = (f32[2,2,32,128]{3,2,1,0:T(8,128)S(1)}, f32[2,2,32,128]{3,2,1,0:T(8,128)S(1)}, u32[]{:S(2)}, u32[]{:S(2)}) collective-permute-start(f32[2,2,32,128]{3,2,1,0:T(8,128)S(1)} %get-tuple-element.60), channel_id=1, source_target_pairs={{1,2},{3,4},{5,6},{7,0},{2,1},{4,3},{6,5},{0,7},{9,10},{11,12},{13... | collective-permute-start | bytes 196616 | tf_op jit(solution)/shard_map/ppermute | solution.py:83
  61.4 0.0 collective-permute-start.12
  61.4 1.5 %collective-permute-start.9 = (f32[2,2,16,128]{3,2,1,0:T(8,128)S(1)}, f32[2,2,16,128]{3,2,1,0:T(8,128)S(1)}, u32[]{:S(2)}, u32[]{:S(2)}) collective-permute-start(f32[2,2,16,128]{3,2,1,0:T(8,128)S(1)} %get-tuple-element.58), channel_id=1, source_target_pairs={{2,4},{3,5},{6,0},{7,1},{4,2},{5,3},{0,6},{1,7},{10,12},{11,13},{1... | collective-permute-start | bytes 98312 | tf_op jit(solution)/shard_map/ppermute | solution.py:83
  62.9 0.4 collective-permute-start.10
  63.3 3.2 %collective-permute-done.9.beyond_far = f32[2,2,16,128]{3,2,1,0:T(8,128)S(1)} collective-permute-done((f32[2,2,16,128]{3,2,1,0:T(8,128)S(1)}, f32[2,2,16,128]{3,2,1,0:T(8,128)S(1)}, u32[]{:S(2)}, u32[]{:S(2)}) %collective-permute-start.9) | collective-permute-done | bytes 32800 | tf_op jit(solution)/shard_map/ppermute | solution.py:83
  66.5 0.3 collective-permute-done.10.beyond_near
  66.8 0.0 collective-permute-done.11.from_far
  66.8 0.0 collective-permute-done.12.from_near
  66.8 3.3 %shard_map.94 = (f32[2,256,256]{2,1,0:T(8,128)S(1)}, bf16[2,2,16,256]{3,2,1,0:T(8,128)(2,1)S(1)}, bf16[2,2,16,256]{3,2,1,0:T(8,128)(2,1)S(1)}, f32[2,2,16,128]{3,2,1,0:T(8,128)}) custom-call(s32[1]{0:T(128)} %bitcast.place_ref, s32[128]{0:T(128)S(1)} %get-tuple-element.39.table_ref, f32[2,2,48,128]{3,2,1,0:T(8,128)S(1)} %get-tuple-element.57.sums_ref, ...), custom_call_target="tpu_custom_call" | custom-call | tf_op jit(solution)/shard_map/pallas_call | solution.py:52
  70.1 0.8 collective-permute-start.13
  70.9 0.0 collective-permute-start.14
  70.9 3.7 %shard_map.95.inner_ref = f32[2,256,256]{2,1,0:T(8,128)S(1)} custom-call(s32[1]{0:T(128)} %bitcast.place_ref, f32[2,256,256]{2,1,0:T(8,128)S(1)} %get-tuple-element.65.mid_ref, f32[2,6,8,256]{3,2,1,0:T(8,128)S(1)} %collective-permute-done.1.far_ref.base_far_ref.thin_far, f32[2,256,256]{2,1,0:T(8,128)S(1)} %get-tuple-element.42.base_ref, ...), custom_call_target="tpu_custom_call" | custom-call | tf_op jit(solution)/shard_map/pallas_call | solution.py:52
  74.6 0.1 collective-permute-done.13.far_ref
  74.7 0.0 collective-permute-done.14.near_ref
  74.7 4.4 %shard_map.96 = (f32[2,256,256]{2,1,0:T(8,128)S(1)}, f32[2,2,48,128]{3,2,1,0:T(8,128)S(1)}, f32[2,2,32,128]{3,2,1,0:T(8,128)S(1)}, f32[2,2,32,128]{3,2,1,0:T(8,1...) custom-call(s32[1]{0:T(128)} %bitcast.place_ref, s32[128]{0:T(128)S(1)} %get-tuple-element.39.table_ref, ...), custom_call_target="tpu_custom_call" | custom-call | tf_op jit(solution)/shard_map/pallas_call | solution.py:52
  79.1 2.2 %collective-permute-start.17 = (f32[2,2,32,128]{3,2,1,0:T(8,128)S(1)}, f32[2,2,32,128]{3,2,1,0:T(8,128)S(1)}, u32[]{:S(2)}, u32[]{:S(2)}) collective-permute-start(f32[2,2,32,128]{3,2,1,0:T(8,128)S(1)} %get-tuple-element.69), channel_id=1, source_target_pairs={{1,2},{3,4},{5,6},{7,0},{2,1},{4,3},{6,5},{0,7},{9,10},{11,12},{13... | collective-permute-start | bytes 196616 | tf_op jit(solution)/shard_map/ppermute | solution.py:83
  81.3 0.0 collective-permute-start.18
  81.4 1.2 %collective-permute-start.15 = (f32[2,2,16,128]{3,2,1,0:T(8,128)S(1)}, f32[2,2,16,128]{3,2,1,0:T(8,128)S(1)}, u32[]{:S(2)}, u32[]{:S(2)}) collective-permute-start(f32[2,2,16,128]{3,2,1,0:T(8,128)S(1)} %get-tuple-element.67), channel_id=1, source_target_pairs={{2,4},{3,5},{6,0},{7,1},{4,2},{5,3},{0,6},{1,7},{10,12},{11,13},{1... | collective-permute-start | bytes 98312 | tf_op jit(solution)/shard_map/ppermute | solution.py:83
  82.5 0.7 collective-permute-start.16
  83.3 3.2 %collective-permute-done.15.beyond_far = f32[2,2,16,128]{3,2,1,0:T(8,128)S(1)} collective-permute-done((f32[2,2,16,128]{3,2,1,0:T(8,128)S(1)}, f32[2,2,16,128]{3,2,1,0:T(8,128)S(1)}, u32[]{:S(2)}, u32[]{:S(2)}) %collective-permute-start.15) | collective-permute-done | bytes 32800 | tf_op jit(solution)/shard_map/ppermute | solution.py:83
  86.5 0.0 collective-permute-done.16.beyond_near
  86.5 0.0 collective-permute-done.17.from_far
  86.5 0.0 collective-permute-done.18.from_near
  86.5 3.3 %shard_map.97 = (f32[2,256,256]{2,1,0:T(8,128)S(1)}, bf16[2,2,16,256]{3,2,1,0:T(8,128)(2,1)S(1)}, bf16[2,2,16,256]{3,2,1,0:T(8,128)(2,1)S(1)}, f32[2,2,16,128]{3,2,1,0:T(8,128)S(1)}) custom-call(s32[1]{0:T(128)} %bitcast.place_ref, s32[128]{0:T(128)S(1)} %get-tuple-element.39.table_ref, f32[2,2,48,128]{3,2,1,0:T(8,128)S(1)} %get-tuple-element.66.sums_ref, ...), custom_call_target="tpu_custom_call" | custom-call | tf_op jit(solution)/shard_map/pallas_call | solution.py:52
  89.8 1.0 collective-permute-start.19
  90.7 0.0 collective-permute-start.20
  90.7 3.0 %shard_map.98.inner_ref = f32[16,2,32,128]{3,2,1,0:T(8,128)S(1)} custom-call(s32[1]{0:T(128)} %bitcast.place_ref, f32[2,256,256]{2,1,0:T(8,128)S(1)} %get-tuple-element.74.mid_ref), custom_call_target="tpu_custom_call" | custom-call | tf_op jit(solution)/shard_map/pallas_call | solution.py:52
  93.7 0.7 collective-permute-done.19.far_ref
  94.4 1.9 %shard_map.99 = f32[16,2,32,128]{3,2,1,0:T(8,128)} custom-call(s32[1]{0:T(128)} %bitcast.place_ref, bf16[2,2,16,256]{3,2,1,0:T(8,128)(2,1)S(1)} %collective-permute-done.19.far_ref, bf16[2,2,16,256]{3,2,1,0:T(8,128)(2,1)S(1)} %collective-permute-done.20.near_ref, f32[16,2,32,128]{3,2,1,0:T(8,128)S(1)} %shard_map.98.inner_ref), custom_call_target="tpu_custom_call" | custom-call | tf_op jit(solution)/shard_map/pallas_call | solution.py:52
  96.3 6.2 %all-to-all-start.1 = ((f32[16,2,32,128]{3,2,1,0:T(8,128)}), f32[16,2,32,128]{3,2,1,0:T(8,128)S(1)}, u32[]{:S(2)}, u32[]{:S(2)}) async-start(f32[16,2,32,128]{3,2,1,0:T(8,128)} %shard_map.99), calls=%async_computation.1 | async-start | bytes 1048576 | tf_op jit(solution)/shard_map/all_to_all | solution.py:806
  102.6 3.5 %collective-permute-start.21 = (f32[2,16,128]{2,1,0:T(8,128)S(1)}, f32[2,16,128]{2,1,0:T(8,128)S(1)}, u32[]{:S(2)}, u32[]{:S(2)}) collective-permute-start(f32[2,16,128]{2,1,0:T(8,128)S(1)} %get-tuple-element.79), channel_id=1, source_target_pairs={{0,8},{8,0},{1,9},{9,1},{2,10},{10,2},{3,11},{11,3},{4,12},{12,4},... | collective-permute-start | bytes 49160 | tf_op jit(solution)/shard_map/ppermute | solution.py:88
  106.1 6.3 %collective-permute-done.21 = f32[2,16,128]{2,1,0:T(8,128)S(1)} collective-permute-done((f32[2,16,128]{2,1,0:T(8,128)S(1)}, f32[2,16,128]{2,1,0:T(8,128)S(1)}, u32[]{:S(2)}, u32[]{:S(2)}) %collective-permute-start.21) | collective-permute-done | bytes 16416 | tf_op jit(solution)/shard_map/ppermute | solution.py:88
  112.4 0.6 maximum_select_fusion.1
  113.0 0.9 all-to-all-done.1
  113.9 0.8 copy.10
  (9 shorter events, 0.1 us)
Async XLA Ops:
  0.6 10.8 %copy-start = (f32[2,2,4,512]{3,2,1,0:T(4,128)S(1)}, f32[2,2,4,512]{3,2,1,0:T(4,128)}, u32[]{:S(2)}) copy-start(f32[2,2,4,512]{3,2,1,0:T(4,128)} %param.13) | copy-start | bytes 98308
  4.3 25.4 %all-to-all-start = ((bf16[16,304,128]{2,1,0:T(8,128)(2,1)}), bf16[16,304,128]{2,1,0:T(8,128)(2,1)S(1)}, u32[]{:S(2)}, u32[]{:S(2)}) async-start(bf16[16,304,128]{2,1,0:T(8,128)(2,1)} %shard_map.86), calls=%async_computation | async-start | bytes 2490368 | tf_op jit(solution)/shard_map/all_to_all | solution.py:740
  11.5 17.5 %collective-permute-start = (f32[2,16,128]{2,1,0:T(8,128)S(1)}, f32[2,16,128]{2,1,0:T(8,128)S(1)}, u32[]{:S(2)}, u32[]{:S(2)}) collective-permute-start(f32[2,16,128]{2,1,0:T(8,128)S(1)} %get-tuple-element.81), channel_id=1, source_target_pairs={{0,8},{8,0},{1,9},{9,1},{2,10},{10,2},{3,11},{11,3},{4,12},{12,4},... | collective-permute-start | bytes 49160 | tf_op jit(solution)/shard_map/ppermute | solution.py:88
  30.0 5.3 %collective-permute-start.1 = (f32[2,6,8,256]{3,2,1,0:T(8,128)S(1)}, f32[2,6,8,256]{3,2,1,0:T(8,128)S(1)}, u32[]{:S(2)}, u32[]{:S(2)}) collective-permute-start(f32[2,6,8,256]{3,2,1,0:T(8,128)S(1)} %get-tuple-element.40), channel_id=1, source_target_pairs={{1,2},{3,4},{5,6},{7,0},{2,1},{4,3},{6,5},{0,7},{9,10},{11,12},{13... | collective-permute-start | bytes 294920 | tf_op jit(solution)/shard_map/ppermute | solution.py:83
  32.0 3.3 %collective-permute-start.2 = (f32[2,6,8,256]{3,2,1,0:T(8,128)S(1)}, f32[2,6,8,256]{3,2,1,0:T(8,128)S(1)}, u32[]{:S(2)}, u32[]{:S(2)}) collective-permute-start(f32[2,6,8,256]{3,2,1,0:T(8,128)S(1)} %get-tuple-element.41), channel_id=1, source_target_pairs={{0,1},{2,3},{4,5},{6,7},{1,0},{3,2},{5,4},{7,6},{8,9},{10,11},{12,... | collective-permute-start | bytes 294920 | tf_op jit(solution)/shard_map/ppermute | solution.py:83
  39.5 7.4 %collective-permute-start.5 = (f32[2,2,32,128]{3,2,1,0:T(8,128)S(1)}, f32[2,2,32,128]{3,2,1,0:T(8,128)S(1)}, u32[]{:S(2)}, u32[]{:S(2)}) collective-permute-start(f32[2,2,32,128]{3,2,1,0:T(8,128)S(1)} %get-tuple-element.49), channel_id=1, source_target_pairs={{1,2},{3,4},{5,6},{7,0},{2,1},{4,3},{6,5},{0,7},{9,10},{11,12},{13... | collective-permute-start | bytes 196616 | tf_op jit(solution)/shard_map/ppermute | solution.py:83
  41.5 5.4 %collective-permute-start.6 = (f32[2,2,32,128]{3,2,1,0:T(8,128)S(1)}, f32[2,2,32,128]{3,2,1,0:T(8,128)S(1)}, u32[]{:S(2)}, u32[]{:S(2)}) collective-permute-start(f32[2,2,32,128]{3,2,1,0:T(8,128)S(1)} %get-tuple-element.50), channel_id=1, source_target_pairs={{0,1},{2,3},{4,5},{6,7},{1,0},{3,2},{5,4},{7,6},{8,9},{10,11},{12,... | collective-permute-start | bytes 196616 | tf_op jit(solution)/shard_map/ppermute | solution.py:83
  41.5 5.1 %collective-permute-start.3 = (f32[2,2,16,128]{3,2,1,0:T(8,128)S(1)}, f32[2,2,16,128]{3,2,1,0:T(8,128)S(1)}, u32[]{:S(2)}, u32[]{:S(2)}) collective-permute-start(f32[2,2,16,128]{3,2,1,0:T(8,128)S(1)} %get-tuple-element.47), channel_id=1, source_target_pairs={{2,4},{3,5},{6,0},{7,1},{4,2},{5,3},{0,6},{1,7},{10,12},{11,13},{1... | collective-permute-start | bytes 98312 | tf_op jit(solution)/shard_map/ppermute | solution.py:83
  43.0 3.9 %collective-permute-start.4 = (f32[2,2,16,128]{3,2,1,0:T(8,128)S(1)}, f32[2,2,16,128]{3,2,1,0:T(8,128)S(1)}, u32[]{:S(2)}, u32[]{:S(2)}) collective-permute-start(f32[2,2,16,128]{3,2,1,0:T(8,128)S(1)} %get-tuple-element.48), channel_id=1, source_target_pairs={{0,2},{1,3},{4,6},{5,7},{2,0},{3,1},{6,4},{7,5},{8,10},{9,11},{12,... | collective-permute-start | bytes 98312 | tf_op jit(solution)/shard_map/ppermute | solution.py:83
  50.1 4.9 %collective-permute-start.7 = (bf16[2,2,16,256]{3,2,1,0:T(8,128)(2,1)S(1)}, bf16[2,2,16,256]{3,2,1,0:T(8,128)(2,1)S(1)}, u32[]{:S(2)}, u32[]{:S(2)}) collective-permute-start(bf16[2,2,16,256]{3,2,1,0:T(8,128)(2,1)S(1)} %get-tuple-element.54), channel_id=1, source_target_pairs={{1,2},{3,4},{5,6},{7,0},{2,1},{4,3},{6,5},{0,7},{9,10},{11,12},{13... | collective-permute-start | bytes 98312 | tf_op jit(solution)/shard_map/ppermute | solution.py:83
  51.0 4.1 %collective-permute-start.8 = (bf16[2,2,16,256]{3,2,1,0:T(8,128)(2,1)S(1)}, bf16[2,2,16,256]{3,2,1,0:T(8,128)(2,1)S(1)}, u32[]{:S(2)}, u32[]{:S(2)}) collective-permute-start(bf16[2,2,16,256]{3,2,1,0:T(8,128)(2,1)S(1)} %get-tuple-element.55), channel_id=1, source_target_pairs={{0,1},{2,3},{4,5},{6,7},{1,0},{3,2},{5,4},{7,6},{8,9},{10,11},{12,... | collective-permute-start | bytes 98312 | tf_op jit(solution)/shard_map/ppermute | solution.py:83
  59.5 7.4 %collective-permute-start.11 = (f32[2,2,32,128]{3,2,1,0:T(8,128)S(1)}, f32[2,2,32,128]{3,2,1,0:T(8,128)S(1)}, u32[]{:S(2)}, u32[]{:S(2)}) collective-permute-start(f32[2,2,32,128]{3,2,1,0:T(8,128)S(1)} %get-tuple-element.60), channel_id=1, source_target_pairs={{1,2},{3,4},{5,6},{7,0},{2,1},{4,3},{6,5},{0,7},{9,10},{11,12},{13... | collective-permute-start | bytes 196616 | tf_op jit(solution)/shard_map/ppermute | solution.py:83
  61.4 5.4 %collective-permute-start.12 = (f32[2,2,32,128]{3,2,1,0:T(8,128)S(1)}, f32[2,2,32,128]{3,2,1,0:T(8,128)S(1)}, u32[]{:S(2)}, u32[]{:S(2)}) collective-permute-start(f32[2,2,32,128]{3,2,1,0:T(8,128)S(1)} %get-tuple-element.61), channel_id=1, source_target_pairs={{0,1},{2,3},{4,5},{6,7},{1,0},{3,2},{5,4},{7,6},{8,9},{10,11},{12,... | collective-permute-start | bytes 196616 | tf_op jit(solution)/shard_map/ppermute | solution.py:83
  61.4 5.1 %collective-permute-start.9 = (f32[2,2,16,128]{3,2,1,0:T(8,128)S(1)}, f32[2,2,16,128]{3,2,1,0:T(8,128)S(1)}, u32[]{:S(2)}, u32[]{:S(2)}) collective-permute-start(f32[2,2,16,128]{3,2,1,0:T(8,128)S(1)} %get-tuple-element.58), channel_id=1, source_target_pairs={{2,4},{3,5},{6,0},{7,1},{4,2},{5,3},{0,6},{1,7},{10,12},{11,13},{1... | collective-permute-start | bytes 98312 | tf_op jit(solution)/shard_map/ppermute | solution.py:83
  62.9 3.9 %collective-permute-start.10 = (f32[2,2,16,128]{3,2,1,0:T(8,128)S(1)}, f32[2,2,16,128]{3,2,1,0:T(8,128)S(1)}, u32[]{:S(2)}, u32[]{:S(2)}) collective-permute-start(f32[2,2,16,128]{3,2,1,0:T(8,128)S(1)} %get-tuple-element.59), channel_id=1, source_target_pairs={{0,2},{1,3},{4,6},{5,7},{2,0},{3,1},{6,4},{7,5},{8,10},{9,11},{12,... | collective-permute-start | bytes 98312 | tf_op jit(solution)/shard_map/ppermute | solution.py:83
  70.1 4.6 %collective-permute-start.13 = (bf16[2,2,16,256]{3,2,1,0:T(8,128)(2,1)S(1)}, bf16[2,2,16,256]{3,2,1,0:T(8,128)(2,1)S(1)}, u32[]{:S(2)}, u32[]{:S(2)}) collective-permute-start(bf16[2,2,16,256]{3,2,1,0:T(8,128)(2,1)S(1)} %get-tuple-element.63), channel_id=1, source_target_pairs={{1,2},{3,4},{5,6},{7,0},{2,1},{4,3},{6,5},{0,7},{9,10},{11,12},{13... | collective-permute-start | bytes 98312 | tf_op jit(solution)/shard_map/ppermute | solution.py:83
  70.9 3.9 %collective-permute-start.14 = (bf16[2,2,16,256]{3,2,1,0:T(8,128)(2,1)S(1)}, bf16[2,2,16,256]{3,2,1,0:T(8,128)(2,1)S(1)}, u32[]{:S(2)}, u32[]{:S(2)}) collective-permute-start(bf16[2,2,16,256]{3,2,1,0:T(8,128)(2,1)S(1)} %get-tuple-element.64), channel_id=1, source_target_pairs={{0,1},{2,3},{4,5},{6,7},{1,0},{3,2},{5,4},{7,6},{8,9},{10,11},{12,... | collective-permute-start | bytes 98312 | tf_op jit(solution)/shard_map/ppermute | solution.py:83
  79.1 7.4 %collective-permute-start.17 = (f32[2,2,32,128]{3,2,1,0:T(8,128)S(1)}, f32[2,2,32,128]{3,2,1,0:T(8,128)S(1)}, u32[]{:S(2)}, u32[]{:S(2)}) collective-permute-start(f32[2,2,32,128]{3,2,1,0:T(8,128)S(1)} %get-tuple-element.69), channel_id=1, source_target_pairs={{1,2},{3,4},{5,6},{7,0},{2,1},{4,3},{6,5},{0,7},{9,10},{11,12},{13... | collective-permute-start | bytes 196616 | tf_op jit(solution)/shard_map/ppermute | solution.py:83
  81.3 5.1 %collective-permute-start.18 = (f32[2,2,32,128]{3,2,1,0:T(8,128)S(1)}, f32[2,2,32,128]{3,2,1,0:T(8,128)S(1)}, u32[]{:S(2)}, u32[]{:S(2)}) collective-permute-start(f32[2,2,32,128]{3,2,1,0:T(8,128)S(1)} %get-tuple-element.70), channel_id=1, source_target_pairs={{0,1},{2,3},{4,5},{6,7},{1,0},{3,2},{5,4},{7,6},{8,9},{10,11},{12,... | collective-permute-start | bytes 196616 | tf_op jit(solution)/shard_map/ppermute | solution.py:83
  81.4 5.1 %collective-permute-start.15 = (f32[2,2,16,128]{3,2,1,0:T(8,128)S(1)}, f32[2,2,16,128]{3,2,1,0:T(8,128)S(1)}, u32[]{:S(2)}, u32[]{:S(2)}) collective-permute-start(f32[2,2,16,128]{3,2,1,0:T(8,128)S(1)} %get-tuple-element.67), channel_id=1, source_target_pairs={{2,4},{3,5},{6,0},{7,1},{4,2},{5,3},{0,6},{1,7},{10,12},{11,13},{1... | collective-permute-start | bytes 98312 | tf_op jit(solution)/shard_map/ppermute | solution.py:83
  82.5 3.9 %collective-permute-start.16 = (f32[2,2,16,128]{3,2,1,0:T(8,128)S(1)}, f32[2,2,16,128]{3,2,1,0:T(8,128)S(1)}, u32[]{:S(2)}, u32[]{:S(2)}) collective-permute-start(f32[2,2,16,128]{3,2,1,0:T(8,128)S(1)} %get-tuple-element.68), channel_id=1, source_target_pairs={{0,2},{1,3},{4,6},{5,7},{2,0},{3,1},{6,4},{7,5},{8,10},{9,11},{12,... | collective-permute-start | bytes 98312 | tf_op jit(solution)/shard_map/ppermute | solution.py:83
  89.8 4.6 %collective-permute-start.19 = (bf16[2,2,16,256]{3,2,1,0:T(8,128)(2,1)S(1)}, bf16[2,2,16,256]{3,2,1,0:T(8,128)(2,1)S(1)}, u32[]{:S(2)}, u32[]{:S(2)}) collective-permute-start(bf16[2,2,16,256]{3,2,1,0:T(8,128)(2,1)S(1)} %get-tuple-element.72), channel_id=1, source_target_pairs={{1,2},{3,4},{5,6},{7,0},{2,1},{4,3},{6,5},{0,7},{9,10},{11,12},{13... | collective-permute-start | bytes 98312 | tf_op jit(solution)/shard_map/ppermute | solution.py:83
  90.7 3.7 %collective-permute-start.20 = (bf16[2,2,16,256]{3,2,1,0:T(8,128)(2,1)S(1)}, bf16[2,2,16,256]{3,2,1,0:T(8,128)(2,1)S(1)}, u32[]{:S(2)}, u32[]{:S(2)}) collective-permute-start(bf16[2,2,16,256]{3,2,1,0:T(8,128)(2,1)S(1)} %get-tuple-element.73), channel_id=1, source_target_pairs={{0,1},{2,3},{4,5},{6,7},{1,0},{3,2},{5,4},{7,6},{8,9},{10,11},{12,... | collective-permute-start | bytes 98312 | tf_op jit(solution)/shard_map/ppermute | solution.py:83
  96.3 17.6 %all-to-all-start.1 = ((f32[16,2,32,128]{3,2,1,0:T(8,128)}), f32[16,2,32,128]{3,2,1,0:T(8,128)S(1)}, u32[]{:S(2)}, u32[]{:S(2)}) async-start(f32[16,2,32,128]{3,2,1,0:T(8,128)} %shard_map.99), calls=%async_computation.1 | async-start | bytes 1048576 | tf_op jit(solution)/shard_map/all_to_all | solution.py:806
  102.6 9.8 %collective-permute-start.21 = (f32[2,16,128]{2,1,0:T(8,128)S(1)}, f32[2,16,128]{2,1,0:T(8,128)S(1)}, u32[]{:S(2)}, u32[]{:S(2)}) collective-permute-start(f32[2,16,128]{2,1,0:T(8,128)S(1)} %get-tuple-element.79), channel_id=1, source_target_pairs={{0,8},{8,0},{1,9},{9,1},{2,10},{10,2},{3,11},{11,3},{4,12},{12,4},... | collective-permute-start | bytes 49160 | tf_op jit(solution)/shard_map/ppermute | solution.py:88

commit v2 on v0

--- a/solution.py
+++ b/solution.py
@@ -94,13 +94,15 @@
 
 
 def row_next(x):
-    lane = lax.broadcasted_iota(I32, x.shape, 1)
-    return jnp.where(lane == NROW - 1, 0.0, pltpu.roll(x, NROW - 1, 1))
+    low, high = (pltpu.roll(half, COLS - 1, 1) for half in (x[:, :COLS], x[:, COLS:]))
+    inner = lax.broadcasted_iota(I32, low.shape, 1) < COLS - 1
+    return jnp.concatenate([jnp.where(inner, low, high), jnp.where(inner, high, 0.0)], axis=1)
 
 
 def row_prev(x):
-    lane = lax.broadcasted_iota(I32, x.shape, 1)
-    return jnp.where(lane == 0, 0.0, pltpu.roll(x, 1, 1))
+    low, high = (pltpu.roll(half, 1, 1) for half in (x[:, :COLS], x[:, COLS:]))
+    inner = lax.broadcasted_iota(I32, low.shape, 1) > 0
+    return jnp.concatenate([jnp.where(inner, low, 0.0), jnp.where(inner, high, low)], axis=1)
 
 
 def col_next(x):

time: 115 us -> 114 us (level)
  waiting for transfers between devices: 31.5 us -> 33.1 us
  starting transfers between devices: 37.5 us -> 36.2 us
  Pallas kernels: 42 us -> 40.8 us
    ppermute x20, waiting for transfers between devices: 9.69 us -> 11.9 us  [exchanged(): results.append(lax.ppermute(value, 'zc', pairs))]
    ppermute x20, starting transfers between devices: 17.1 us -> 15.9 us  [exchanged(): results.append(lax.ppermute(value, 'zc', pairs))]
    pallas_call x15, Pallas kernels: 42 us -> 40.8 us  [call(): pl.pallas_call(body, out_shape=outs, in_specs=[spaces.get(n, VMEM) for n...]
  transfers between devices with their start and end apart: 24 -> 24, of which waited for: 11 -> 13; matrix products, arithmetic and copies ran while one was open for 1% -> 1% of each run, Pallas kernels for 13% -> 12%
where the time goes in v2:
time: 114 us
  Pallas kernels  40.8 us (36%)
  starting transfers between devices  36.2 us (32%)
  waiting for transfers between devices  33.1 us (29%)
  local copies, waits for them, and re-layouts  2.16 us (2%)
    pallas_call x15, Pallas kernels, call(): pl.pallas_call(body, out_shape=outs, in_specs=[spaces.get(n, VMEM) for n...  40.8 us
    ppermute x2, waiting for transfers between devices, swapped(): return lax.ppermute(value, 'xh', [(0, 1), (1, 0)])  19.6 us
    ppermute x20, starting transfers between devices, exchanged(): results.append(lax.ppermute(value, 'zc', pairs))  15.9 us
    ppermute x20, waiting for transfers between devices, exchanged(): results.append(lax.ppermute(value, 'zc', pairs))  11.9 us
    all_to_all x1, starting transfers between devices, on_device(): got = lax.all_to_all(packed, whole, split_axis=0, concat_axis=0, tiled=True)  7.13 us
    ppermute x2, starting transfers between devices, swapped(): return lax.ppermute(value, 'xh', [(0, 1), (1, 0)])  6.99 us
    all_to_all x1, starting transfers between devices, on_device(): back = lax.all_to_all(done, whole, split_axis=0, concat_axis=0, tiled=True)  6.17 us
  transfers between devices with their start and end apart: 24, of which 13 were waited for; matrix products, arithmetic and copies ran while one was open for 1% of the time, Pallas kernels for 12%

profile of v2, /device:TPU:0, one launch (start us, length us, event | category | flops | bytes accessed | tf_op | source)
XLA Modules:
  0.0 113.8 jit_solution(491234215111403082)
XLA Ops:
  0.6 1.3 %copy.9.count_hbm = s32[1,1,3,8]{3,2,1,0:T(4,128)} copy(s32[1,1,3,8]{3,1,2,0:T(1,128)} %param.11) | data formatting | bytes 192 | tf_op args[4]
  1.9 2.4 %shard_map.86 = bf16[16,304,128]{2,1,0:T(8,128)(2,1)} custom-call(s32[1,1,3,8]{3,2,1,0:T(4,128)} %copy.9.count_hbm, f32[2,16,32,128]{3,2,1,0:T(8,128)} %adj_hbm.1, bf16[2,16,32,128]{3,2,1,0:T(8,128)(2,1)} %base_hbm.1, s32[3,8,128]{2,1,0:T(8,128)} %bitcast.15, s32[3,8,128]{2,1,0:T(8,128)} %bitcast.16, f32[3,8,16,128]{3,2,1,0:T(8,128)} %bitcast.13), custom_call_target="tpu_custom_call" | custom-call | tf_op jit(solution)/shard_map/pallas_call | solution.py:52
  4.3 7.1 %all-to-all-start = ((bf16[16,304,128]{2,1,0:T(8,128)(2,1)}), bf16[16,304,128]{2,1,0:T(8,128)(2,1)S(1)}, u32[]{:S(2)}, u32[]{:S(2)}) async-start(bf16[16,304,128]{2,1,0:T(8,128)(2,1)} %shard_map.86), calls=%async_computation | async-start | bytes 2490368 | tf_op jit(solution)/shard_map/all_to_all | solution.py:733
  11.5 3.5 %collective-permute-start = (f32[2,16,128]{2,1,0:T(8,128)S(1)}, f32[2,16,128]{2,1,0:T(8,128)S(1)}, u32[]{:S(2)}, u32[]{:S(2)}) collective-permute-start(f32[2,16,128]{2,1,0:T(8,128)S(1)} %get-tuple-element.81), channel_id=1, source_target_pairs={{0,8},{8,0},{1,9},{9,1},{2,10},{10,2},{3,11},{11,3},{4,12},{12,4},... | collective-permute-start | bytes 49160 | tf_op jit(solution)/shard_map/ppermute | solution.py:88
  15.0 14.0 %collective-permute-done = f32[2,16,128]{2,1,0:T(8,128)S(1)} collective-permute-done((f32[2,16,128]{2,1,0:T(8,128)S(1)}, f32[2,16,128]{2,1,0:T(8,128)S(1)}, u32[]{:S(2)}, u32[]{:S(2)}) %collective-permute-start) | collective-permute-done | bytes 16416 | tf_op jit(solution)/shard_map/ppermute | solution.py:88
  29.0 0.7 all-to-all-done.got_ref
  29.7 0.3 shard_map.88
  30.0 2.0 %collective-permute-start.1 = (f32[2,6,8,256]{3,2,1,0:T(8,128)S(1)}, f32[2,6,8,256]{3,2,1,0:T(8,128)S(1)}, u32[]{:S(2)}, u32[]{:S(2)}) collective-permute-start(f32[2,6,8,256]{3,2,1,0:T(8,128)S(1)} %get-tuple-element.40), channel_id=1, source_target_pairs={{1,2},{3,4},{5,6},{7,0},{2,1},{4,3},{6,5},{0,7},{9,10},{11,12},{13... | collective-permute-start | bytes 294920 | tf_op jit(solution)/shard_map/ppermute | solution.py:83
  32.0 0.1 collective-permute-start.2
  32.1 1.0 shard_map.89.inner_ref
  33.1 2.5 %shard_map.87 = (s32[49,8,128]{2,1,0:T(8,128)S(1)}, f32[49,16,128]{2,1,0:T(8,128)S(1)}, s32[128]{0:T(128)S(1)}) custom-call(bf16[16,304,128]{2,1,0:T(8,128)(2,1)S(1)} %all-to-all-done.got_ref), custom_call_target="tpu_custom_call" | custom-call | tf_op jit(solution)/shard_map/pallas_call | solution.py:52
  35.6 0.0 collective-permute-done.1.far_ref.base_far_ref.thin_far
  35.6 0.0 collective-permute-done.2.near_ref.base_near_ref.thin_near
  35.7 3.5 %shard_map.90 = (f32[2,256,256]{2,1,0:T(8,128)S(1)}, f32[2,2,48,128]{3,2,1,0:T(8,128)S(1)}, f32[2,2,32,128]{3,2,1,0:T(8,128)S(1)}, f32[2,2,32,128]{3,2,1,0:T(8,1...) custom-call(s32[1]{0:T(128)} %bitcast.place_ref, s32[128]{0:T(128)S(1)} %get-tuple-element.39.table_ref, ...), custom_call_target="tpu_custom_call" | custom-call | tf_op jit(solution)/shard_map/pallas_call | solution.py:52
  39.2 2.3 %collective-permute-start.5 = (f32[2,2,32,128]{3,2,1,0:T(8,128)S(1)}, f32[2,2,32,128]{3,2,1,0:T(8,128)S(1)}, u32[]{:S(2)}, u32[]{:S(2)}) collective-permute-start(f32[2,2,32,128]{3,2,1,0:T(8,128)S(1)} %get-tuple-element.49), channel_id=1, source_target_pairs={{1,2},{3,4},{5,6},{7,0},{2,1},{4,3},{6,5},{0,7},{9,10},{11,12},{13... | collective-permute-start | bytes 196616 | tf_op jit(solution)/shard_map/ppermute | solution.py:83
  41.5 0.0 collective-permute-start.6
  41.5 1.5 %collective-permute-start.3 = (f32[2,2,16,128]{3,2,1,0:T(8,128)S(1)}, f32[2,2,16,128]{3,2,1,0:T(8,128)S(1)}, u32[]{:S(2)}, u32[]{:S(2)}) collective-permute-start(f32[2,2,16,128]{3,2,1,0:T(8,128)S(1)} %get-tuple-element.47), channel_id=1, source_target_pairs={{2,4},{3,5},{6,0},{7,1},{4,2},{5,3},{0,6},{1,7},{10,12},{11,13},{1... | collective-permute-start | bytes 98312 | tf_op jit(solution)/shard_map/ppermute | solution.py:83
  43.0 0.3 collective-permute-start.4
  43.3 1.3 %shard_map.91 = (f32[49,128,128]{2,1,0:T(8,128)S(1)}, bf16[49,256,128]{2,1,0:T(8,128)(2,1)S(1)}) custom-call(s32[128]{0:T(128)S(1)} %get-tuple-element.39.table_ref, s32[49,8,128]{2,1,0:T(8,128)S(1)} %get-tuple-element.44.ints_ref, f32[49,16,128]{2,1,0:T(8,128)S(1)} %get-tuple-element.45.weight_ref), custom_call_target="tpu_custom_call" | custom-call | tf_op jit(solution)/shard_map/pallas_call | solution.py:52
  44.6 2.0 %collective-permute-done.3.beyond_far = f32[2,2,16,128]{3,2,1,0:T(8,128)S(1)} collective-permute-done((f32[2,2,16,128]{3,2,1,0:T(8,128)S(1)}, f32[2,2,16,128]{3,2,1,0:T(8,128)S(1)}, u32[]{:S(2)}, u32[]{:S(2)}) %collective-permute-start.3) | collective-permute-done | bytes 32800 | tf_op jit(solution)/shard_map/ppermute | solution.py:83
  46.6 0.3 collective-permute-done.4.beyond_near
  46.9 0.0 collective-permute-done.5.from_far
  46.9 0.0 collective-permute-done.6.from_near
  46.9 3.3 %shard_map.92 = (f32[2,256,256]{2,1,0:T(8,128)S(1)}, bf16[2,2,16,256]{3,2,1,0:T(8,128)(2,1)S(1)}, bf16[2,2,16,256]{3,2,1,0:T(8,128)(2,1)S(1)}, f32[2,2,16,128]{3,2,1,0:T(8,128)}) custom-call(s32[1]{0:T(128)} %bitcast.place_ref, s32[128]{0:T(128)S(1)} %get-tuple-element.39.table_ref, f32[2,2,48,128]{3,2,1,0:T(8,128)S(1)} %get-tuple-element.46.sums_ref, ...), custom_call_target="tpu_custom_call" | custom-call | tf_op jit(solution)/shard_map/pallas_call | solution.py:52
  50.3 0.7 collective-permute-start.7
  51.0 0.0 collective-permute-start.8
  51.0 3.3 %shard_map.93.inner_ref = f32[2,256,256]{2,1,0:T(8,128)S(1)} custom-call(s32[1]{0:T(128)} %bitcast.place_ref, f32[2,256,256]{2,1,0:T(8,128)S(1)} %get-tuple-element.55.mid_ref, f32[2,6,8,256]{3,2,1,0:T(8,128)S(1)} %collective-permute-done.1.far_ref.base_far_ref.thin_far, f32[2,256,256]{2,1,0:T(8,128)S(1)} %get-tuple-element.43.base_ref, ...), custom_call_target="tpu_custom_call" | custom-call | tf_op jit(solution)/shard_map/pallas_call | solution.py:52
  54.4 0.5 collective-permute-done.7.far_ref
  54.9 0.0 collective-permute-done.8.near_ref
  54.9 4.4 %shard_map.94 = (f32[2,256,256]{2,1,0:T(8,128)S(1)}, f32[2,2,48,128]{3,2,1,0:T(8,128)S(1)}, f32[2,2,32,128]{3,2,1,0:T(8,128)S(1)}, f32[2,2,32,128]{3,2,1,0:T(8,1...) custom-call(s32[1]{0:T(128)} %bitcast.place_ref, s32[128]{0:T(128)S(1)} %get-tuple-element.39.table_ref, ...), custom_call_target="tpu_custom_call" | custom-call | tf_op jit(solution)/shard_map/pallas_call | solution.py:52
  59.3 1.8 %collective-permute-start.11 = (f32[2,2,32,128]{3,2,1,0:T(8,128)S(1)}, f32[2,2,32,128]{3,2,1,0:T(8,128)S(1)}, u32[]{:S(2)}, u32[]{:S(2)}) collective-permute-start(f32[2,2,32,128]{3,2,1,0:T(8,128)S(1)} %get-tuple-element.60), channel_id=1, source_target_pairs={{1,2},{3,4},{5,6},{7,0},{2,1},{4,3},{6,5},{0,7},{9,10},{11,12},{13... | collective-permute-start | bytes 196616 | tf_op jit(solution)/shard_map/ppermute | solution.py:83
  61.1 0.0 collective-permute-start.12
  61.1 1.6 %collective-permute-start.9 = (f32[2,2,16,128]{3,2,1,0:T(8,128)S(1)}, f32[2,2,16,128]{3,2,1,0:T(8,128)S(1)}, u32[]{:S(2)}, u32[]{:S(2)}) collective-permute-start(f32[2,2,16,128]{3,2,1,0:T(8,128)S(1)} %get-tuple-element.58), channel_id=1, source_target_pairs={{2,4},{3,5},{6,0},{7,1},{4,2},{5,3},{0,6},{1,7},{10,12},{11,13},{1... | collective-permute-start | bytes 98312 | tf_op jit(solution)/shard_map/ppermute | solution.py:83
  62.7 0.3 collective-permute-start.10
  63.0 3.2 %collective-permute-done.9.beyond_far = f32[2,2,16,128]{3,2,1,0:T(8,128)S(1)} collective-permute-done((f32[2,2,16,128]{3,2,1,0:T(8,128)S(1)}, f32[2,2,16,128]{3,2,1,0:T(8,128)S(1)}, u32[]{:S(2)}, u32[]{:S(2)}) %collective-permute-start.9) | collective-permute-done | bytes 32800 | tf_op jit(solution)/shard_map/ppermute | solution.py:83
  66.2 0.4 collective-permute-done.10.beyond_near
  66.6 0.0 collective-permute-done.11.from_far
  66.6 0.0 collective-permute-done.12.from_near
  66.6 3.3 %shard_map.95 = (f32[2,256,256]{2,1,0:T(8,128)S(1)}, bf16[2,2,16,256]{3,2,1,0:T(8,128)(2,1)S(1)}, bf16[2,2,16,256]{3,2,1,0:T(8,128)(2,1)S(1)}, f32[2,2,16,128]{3,2,1,0:T(8,128)}) custom-call(s32[1]{0:T(128)} %bitcast.place_ref, s32[128]{0:T(128)S(1)} %get-tuple-element.39.table_ref, f32[2,2,48,128]{3,2,1,0:T(8,128)S(1)} %get-tuple-element.57.sums_ref, ...), custom_call_target="tpu_custom_call" | custom-call | tf_op jit(solution)/shard_map/pallas_call | solution.py:52
  69.9 0.7 collective-permute-start.13
  70.7 0.0 collective-permute-start.14
  70.7 3.3 %shard_map.96.inner_ref = f32[2,256,256]{2,1,0:T(8,128)S(1)} custom-call(s32[1]{0:T(128)} %bitcast.place_ref, f32[2,256,256]{2,1,0:T(8,128)S(1)} %get-tuple-element.64.mid_ref, f32[2,6,8,256]{3,2,1,0:T(8,128)S(1)} %collective-permute-done.1.far_ref.base_far_ref.thin_far, f32[2,256,256]{2,1,0:T(8,128)S(1)} %get-tuple-element.43.base_ref, ...), custom_call_target="tpu_custom_call" | custom-call | tf_op jit(solution)/shard_map/pallas_call | solution.py:52
  74.0 0.6 collective-permute-done.13.far_ref
  74.6 0.0 collective-permute-done.14.near_ref
  74.6 4.4 %shard_map.97 = (f32[2,256,256]{2,1,0:T(8,128)S(1)}, f32[2,2,48,128]{3,2,1,0:T(8,128)S(1)}, f32[2,2,32,128]{3,2,1,0:T(8,128)S(1)}, f32[2,2,32,128]{3,2,1,0:T(8,1...) custom-call(s32[1]{0:T(128)} %bitcast.place_ref, s32[128]{0:T(128)S(1)} %get-tuple-element.39.table_ref, ...), custom_call_target="tpu_custom_call" | custom-call | tf_op jit(solution)/shard_map/pallas_call | solution.py:52
  78.9 1.8 %collective-permute-start.17 = (f32[2,2,32,128]{3,2,1,0:T(8,128)S(1)}, f32[2,2,32,128]{3,2,1,0:T(8,128)S(1)}, u32[]{:S(2)}, u32[]{:S(2)}) collective-permute-start(f32[2,2,32,128]{3,2,1,0:T(8,128)S(1)} %get-tuple-element.69), channel_id=1, source_target_pairs={{1,2},{3,4},{5,6},{7,0},{2,1},{4,3},{6,5},{0,7},{9,10},{11,12},{13... | collective-permute-start | bytes 196616 | tf_op jit(solution)/shard_map/ppermute | solution.py:83
  80.8 1.6 %collective-permute-start.15 = (f32[2,2,16,128]{3,2,1,0:T(8,128)S(1)}, f32[2,2,16,128]{3,2,1,0:T(8,128)S(1)}, u32[]{:S(2)}, u32[]{:S(2)}) collective-permute-start(f32[2,2,16,128]{3,2,1,0:T(8,128)S(1)} %get-tuple-element.67), channel_id=1, source_target_pairs={{2,4},{3,5},{6,0},{7,1},{4,2},{5,3},{0,6},{1,7},{10,12},{11,13},{1... | collective-permute-start | bytes 98312 | tf_op jit(solution)/shard_map/ppermute | solution.py:83
  82.4 0.3 collective-permute-start.16
  82.7 3.2 %collective-permute-done.15.beyond_far = f32[2,2,16,128]{3,2,1,0:T(8,128)S(1)} collective-permute-done((f32[2,2,16,128]{3,2,1,0:T(8,128)S(1)}, f32[2,2,16,128]{3,2,1,0:T(8,128)S(1)}, u32[]{:S(2)}, u32[]{:S(2)}) %collective-permute-start.15) | collective-permute-done | bytes 32800 | tf_op jit(solution)/shard_map/ppermute | solution.py:83
  85.9 0.4 collective-permute-done.16.beyond_near
  86.3 0.0 collective-permute-done.17.from_far
  86.3 0.0 collective-permute-done.18.from_near
  86.3 3.3 %shard_map.98 = (f32[2,256,256]{2,1,0:T(8,128)S(1)}, bf16[2,2,16,256]{3,2,1,0:T(8,128)(2,1)S(1)}, bf16[2,2,16,256]{3,2,1,0:T(8,128)(2,1)S(1)}, f32[2,2,16,128]{3,2,1,0:T(8,128)S(1)}) custom-call(s32[1]{0:T(128)} %bitcast.place_ref, s32[128]{0:T(128)S(1)} %get-tuple-element.39.table_ref, f32[2,2,48,128]{3,2,1,0:T(8,128)S(1)} %get-tuple-element.66.sums_ref, ...), custom_call_target="tpu_custom_call" | custom-call | tf_op jit(solution)/shard_map/pallas_call | solution.py:52
  89.6 0.7 collective-permute-start.19
  90.3 2.6 %shard_map.99.inner_ref = f32[16,2,32,128]{3,2,1,0:T(8,128)S(1)} custom-call(s32[1]{0:T(128)} %bitcast.place_ref, f32[2,256,256]{2,1,0:T(8,128)S(1)} %get-tuple-element.74.mid_ref), custom_call_target="tpu_custom_call" | custom-call | tf_op jit(solution)/shard_map/pallas_call | solution.py:52
  93.0 1.3 %collective-permute-done.19.far_ref = bf16[2,2,16,256]{3,2,1,0:T(8,128)(2,1)S(1)} collective-permute-done((bf16[2,2,16,256]{3,2,1,0:T(8,128)(2,1)S(1)}, bf16[2,2,16,256]{3,2,1,0:T(8,128)(2,1)S(1)}, u32[]{:S(2)}, u32[]{:S(2)}) %collective-permute-start.19) | collective-permute-done | bytes 32800 | tf_op jit(solution)/shard_map/ppermute | solution.py:83
  94.3 0.0 collective-permute-done.20.near_ref
  94.3 1.8 %shard_map.100 = f32[16,2,32,128]{3,2,1,0:T(8,128)} custom-call(s32[1]{0:T(128)} %bitcast.place_ref, bf16[2,2,16,256]{3,2,1,0:T(8,128)(2,1)S(1)} %collective-permute-done.19.far_ref, bf16[2,2,16,256]{3,2,1,0:T(8,128)(2,1)S(1)} %collective-permute-done.20.near_ref, f32[16,2,32,128]{3,2,1,0:T(8,128)S(1)} %shard_map.99.inner_ref), custom_call_target="tpu_custom_call" | custom-call | tf_op jit(solution)/shard_map/pallas_call | solution.py:52
  96.1 6.2 %all-to-all-start.1 = ((f32[16,2,32,128]{3,2,1,0:T(8,128)}), f32[16,2,32,128]{3,2,1,0:T(8,128)S(1)}, u32[]{:S(2)}, u32[]{:S(2)}) async-start(f32[16,2,32,128]{3,2,1,0:T(8,128)} %shard_map.100), calls=%async_computation.1 | async-start | bytes 1048576 | tf_op jit(solution)/shard_map/all_to_all | solution.py:799
  102.3 3.5 %collective-permute-start.21 = (f32[2,16,128]{2,1,0:T(8,128)S(1)}, f32[2,16,128]{2,1,0:T(8,128)S(1)}, u32[]{:S(2)}, u32[]{:S(2)}) collective-permute-start(f32[2,16,128]{2,1,0:T(8,128)S(1)} %get-tuple-element.79), channel_id=1, source_target_pairs={{0,8},{8,0},{1,9},{9,1},{2,10},{10,2},{3,11},{11,3},{4,12},{12,4},... | collective-permute-start | bytes 49160 | tf_op jit(solution)/shard_map/ppermute | solution.py:88
  105.8 5.6 %collective-permute-done.21 = f32[2,16,128]{2,1,0:T(8,128)S(1)} collective-permute-done((f32[2,16,128]{2,1,0:T(8,128)S(1)}, f32[2,16,128]{2,1,0:T(8,128)S(1)}, u32[]{:S(2)}, u32[]{:S(2)}) %collective-permute-start.21) | collective-permute-done | bytes 16416 | tf_op jit(solution)/shard_map/ppermute | solution.py:88
  111.4 0.6 maximum_select_fusion.1
  112.0 0.9 all-to-all-done.1
  112.9 0.8 copy.10
  (10 shorter events, 0.1 us)
Async XLA Ops:
  0.6 10.8 %copy-start = (f32[2,2,4,512]{3,2,1,0:T(4,128)S(1)}, f32[2,2,4,512]{3,2,1,0:T(4,128)}, u32[]{:S(2)}) copy-start(f32[2,2,4,512]{3,2,1,0:T(4,128)} %param.13) | copy-start | bytes 98308
  4.3 25.4 %all-to-all-start = ((bf16[16,304,128]{2,1,0:T(8,128)(2,1)}), bf16[16,304,128]{2,1,0:T(8,128)(2,1)S(1)}, u32[]{:S(2)}, u32[]{:S(2)}) async-start(bf16[16,304,128]{2,1,0:T(8,128)(2,1)} %shard_map.86), calls=%async_computation | async-start | bytes 2490368 | tf_op jit(solution)/shard_map/all_to_all | solution.py:733
  11.5 17.5 %collective-permute-start = (f32[2,16,128]{2,1,0:T(8,128)S(1)}, f32[2,16,128]{2,1,0:T(8,128)S(1)}, u32[]{:S(2)}, u32[]{:S(2)}) collective-permute-start(f32[2,16,128]{2,1,0:T(8,128)S(1)} %get-tuple-element.81), channel_id=1, source_target_pairs={{0,8},{8,0},{1,9},{9,1},{2,10},{10,2},{3,11},{11,3},{4,12},{12,4},... | collective-permute-start | bytes 49160 | tf_op jit(solution)/shard_map/ppermute | solution.py:88
  30.0 5.7 %collective-permute-start.1 = (f32[2,6,8,256]{3,2,1,0:T(8,128)S(1)}, f32[2,6,8,256]{3,2,1,0:T(8,128)S(1)}, u32[]{:S(2)}, u32[]{:S(2)}) collective-permute-start(f32[2,6,8,256]{3,2,1,0:T(8,128)S(1)} %get-tuple-element.40), channel_id=1, source_target_pairs={{1,2},{3,4},{5,6},{7,0},{2,1},{4,3},{6,5},{0,7},{9,10},{11,12},{13... | collective-permute-start | bytes 294920 | tf_op jit(solution)/shard_map/ppermute | solution.py:83
  32.0 3.7 %collective-permute-start.2 = (f32[2,6,8,256]{3,2,1,0:T(8,128)S(1)}, f32[2,6,8,256]{3,2,1,0:T(8,128)S(1)}, u32[]{:S(2)}, u32[]{:S(2)}) collective-permute-start(f32[2,6,8,256]{3,2,1,0:T(8,128)S(1)} %get-tuple-element.42), channel_id=1, source_target_pairs={{0,1},{2,3},{4,5},{6,7},{1,0},{3,2},{5,4},{7,6},{8,9},{10,11},{12,... | collective-permute-start | bytes 294920 | tf_op jit(solution)/shard_map/ppermute | solution.py:83
  39.2 7.8 %collective-permute-start.5 = (f32[2,2,32,128]{3,2,1,0:T(8,128)S(1)}, f32[2,2,32,128]{3,2,1,0:T(8,128)S(1)}, u32[]{:S(2)}, u32[]{:S(2)}) collective-permute-start(f32[2,2,32,128]{3,2,1,0:T(8,128)S(1)} %get-tuple-element.49), channel_id=1, source_target_pairs={{1,2},{3,4},{5,6},{7,0},{2,1},{4,3},{6,5},{0,7},{9,10},{11,12},{13... | collective-permute-start | bytes 196616 | tf_op jit(solution)/shard_map/ppermute | solution.py:83
  41.5 5.5 %collective-permute-start.6 = (f32[2,2,32,128]{3,2,1,0:T(8,128)S(1)}, f32[2,2,32,128]{3,2,1,0:T(8,128)S(1)}, u32[]{:S(2)}, u32[]{:S(2)}) collective-permute-start(f32[2,2,32,128]{3,2,1,0:T(8,128)S(1)} %get-tuple-element.50), channel_id=1, source_target_pairs={{0,1},{2,3},{4,5},{6,7},{1,0},{3,2},{5,4},{7,6},{8,9},{10,11},{12,... | collective-permute-start | bytes 196616 | tf_op jit(solution)/shard_map/ppermute | solution.py:83
  41.5 5.1 %collective-permute-start.3 = (f32[2,2,16,128]{3,2,1,0:T(8,128)S(1)}, f32[2,2,16,128]{3,2,1,0:T(8,128)S(1)}, u32[]{:S(2)}, u32[]{:S(2)}) collective-permute-start(f32[2,2,16,128]{3,2,1,0:T(8,128)S(1)} %get-tuple-element.47), channel_id=1, source_target_pairs={{2,4},{3,5},{6,0},{7,1},{4,2},{5,3},{0,6},{1,7},{10,12},{11,13},{1... | collective-permute-start | bytes 98312 | tf_op jit(solution)/shard_map/ppermute | solution.py:83
  43.0 3.9 %collective-permute-start.4 = (f32[2,2,16,128]{3,2,1,0:T(8,128)S(1)}, f32[2,2,16,128]{3,2,1,0:T(8,128)S(1)}, u32[]{:S(2)}, u32[]{:S(2)}) collective-permute-start(f32[2,2,16,128]{3,2,1,0:T(8,128)S(1)} %get-tuple-element.48), channel_id=1, source_target_pairs={{0,2},{1,3},{4,6},{5,7},{2,0},{3,1},{6,4},{7,5},{8,10},{9,11},{12,... | collective-permute-start | bytes 98312 | tf_op jit(solution)/shard_map/ppermute | solution.py:83
  50.3 4.6 %collective-permute-start.7 = (bf16[2,2,16,256]{3,2,1,0:T(8,128)(2,1)S(1)}, bf16[2,2,16,256]{3,2,1,0:T(8,128)(2,1)S(1)}, u32[]{:S(2)}, u32[]{:S(2)}) collective-permute-start(bf16[2,2,16,256]{3,2,1,0:T(8,128)(2,1)S(1)} %get-tuple-element.54), channel_id=1, source_target_pairs={{1,2},{3,4},{5,6},{7,0},{2,1},{4,3},{6,5},{0,7},{9,10},{11,12},{13... | collective-permute-start | bytes 98312 | tf_op jit(solution)/shard_map/ppermute | solution.py:83
  51.0 3.9 %collective-permute-start.8 = (bf16[2,2,16,256]{3,2,1,0:T(8,128)(2,1)S(1)}, bf16[2,2,16,256]{3,2,1,0:T(8,128)(2,1)S(1)}, u32[]{:S(2)}, u32[]{:S(2)}) collective-permute-start(bf16[2,2,16,256]{3,2,1,0:T(8,128)(2,1)S(1)} %get-tuple-element.56), channel_id=1, source_target_pairs={{0,1},{2,3},{4,5},{6,7},{1,0},{3,2},{5,4},{7,6},{8,9},{10,11},{12,... | collective-permute-start | bytes 98312 | tf_op jit(solution)/shard_map/ppermute | solution.py:83
  59.3 7.4 %collective-permute-start.11 = (f32[2,2,32,128]{3,2,1,0:T(8,128)S(1)}, f32[2,2,32,128]{3,2,1,0:T(8,128)S(1)}, u32[]{:S(2)}, u32[]{:S(2)}) collective-permute-start(f32[2,2,32,128]{3,2,1,0:T(8,128)S(1)} %get-tuple-element.60), channel_id=1, source_target_pairs={{1,2},{3,4},{5,6},{7,0},{2,1},{4,3},{6,5},{0,7},{9,10},{11,12},{13... | collective-permute-start | bytes 196616 | tf_op jit(solution)/shard_map/ppermute | solution.py:83
  61.1 5.5 %collective-permute-start.12 = (f32[2,2,32,128]{3,2,1,0:T(8,128)S(1)}, f32[2,2,32,128]{3,2,1,0:T(8,128)S(1)}, u32[]{:S(2)}, u32[]{:S(2)}) collective-permute-start(f32[2,2,32,128]{3,2,1,0:T(8,128)S(1)} %get-tuple-element.61), channel_id=1, source_target_pairs={{0,1},{2,3},{4,5},{6,7},{1,0},{3,2},{5,4},{7,6},{8,9},{10,11},{12,... | collective-permute-start | bytes 196616 | tf_op jit(solution)/shard_map/ppermute | solution.py:83
  61.1 5.1 %collective-permute-start.9 = (f32[2,2,16,128]{3,2,1,0:T(8,128)S(1)}, f32[2,2,16,128]{3,2,1,0:T(8,128)S(1)}, u32[]{:S(2)}, u32[]{:S(2)}) collective-permute-start(f32[2,2,16,128]{3,2,1,0:T(8,128)S(1)} %get-tuple-element.58), channel_id=1, source_target_pairs={{2,4},{3,5},{6,0},{7,1},{4,2},{5,3},{0,6},{1,7},{10,12},{11,13},{1... | collective-permute-start | bytes 98312 | tf_op jit(solution)/shard_map/ppermute | solution.py:83
  62.7 3.9 %collective-permute-start.10 = (f32[2,2,16,128]{3,2,1,0:T(8,128)S(1)}, f32[2,2,16,128]{3,2,1,0:T(8,128)S(1)}, u32[]{:S(2)}, u32[]{:S(2)}) collective-permute-start(f32[2,2,16,128]{3,2,1,0:T(8,128)S(1)} %get-tuple-element.59), channel_id=1, source_target_pairs={{0,2},{1,3},{4,6},{5,7},{2,0},{3,1},{6,4},{7,5},{8,10},{9,11},{12,... | collective-permute-start | bytes 98312 | tf_op jit(solution)/shard_map/ppermute | solution.py:83
  69.9 4.6 %collective-permute-start.13 = (bf16[2,2,16,256]{3,2,1,0:T(8,128)(2,1)S(1)}, bf16[2,2,16,256]{3,2,1,0:T(8,128)(2,1)S(1)}, u32[]{:S(2)}, u32[]{:S(2)}) collective-permute-start(bf16[2,2,16,256]{3,2,1,0:T(8,128)(2,1)S(1)} %get-tuple-element.63), channel_id=1, source_target_pairs={{1,2},{3,4},{5,6},{7,0},{2,1},{4,3},{6,5},{0,7},{9,10},{11,12},{13... | collective-permute-start | bytes 98312 | tf_op jit(solution)/shard_map/ppermute | solution.py:83
  70.7 3.9 %collective-permute-start.14 = (bf16[2,2,16,256]{3,2,1,0:T(8,128)(2,1)S(1)}, bf16[2,2,16,256]{3,2,1,0:T(8,128)(2,1)S(1)}, u32[]{:S(2)}, u32[]{:S(2)}) collective-permute-start(bf16[2,2,16,256]{3,2,1,0:T(8,128)(2,1)S(1)} %get-tuple-element.65), channel_id=1, source_target_pairs={{0,1},{2,3},{4,5},{6,7},{1,0},{3,2},{5,4},{7,6},{8,9},{10,11},{12,... | collective-permute-start | bytes 98312 | tf_op jit(solution)/shard_map/ppermute | solution.py:83
  78.9 7.4 %collective-permute-start.17 = (f32[2,2,32,128]{3,2,1,0:T(8,128)S(1)}, f32[2,2,32,128]{3,2,1,0:T(8,128)S(1)}, u32[]{:S(2)}, u32[]{:S(2)}) collective-permute-start(f32[2,2,32,128]{3,2,1,0:T(8,128)S(1)} %get-tuple-element.69), channel_id=1, source_target_pairs={{1,2},{3,4},{5,6},{7,0},{2,1},{4,3},{6,5},{0,7},{9,10},{11,12},{13... | collective-permute-start | bytes 196616 | tf_op jit(solution)/shard_map/ppermute | solution.py:83
  80.8 5.5 %collective-permute-start.18 = (f32[2,2,32,128]{3,2,1,0:T(8,128)S(1)}, f32[2,2,32,128]{3,2,1,0:T(8,128)S(1)}, u32[]{:S(2)}, u32[]{:S(2)}) collective-permute-start(f32[2,2,32,128]{3,2,1,0:T(8,128)S(1)} %get-tuple-element.70), channel_id=1, source_target_pairs={{0,1},{2,3},{4,5},{6,7},{1,0},{3,2},{5,4},{7,6},{8,9},{10,11},{12,... | collective-permute-start | bytes 196616 | tf_op jit(solution)/shard_map/ppermute | solution.py:83
  80.8 5.1 %collective-permute-start.15 = (f32[2,2,16,128]{3,2,1,0:T(8,128)S(1)}, f32[2,2,16,128]{3,2,1,0:T(8,128)S(1)}, u32[]{:S(2)}, u32[]{:S(2)}) collective-permute-start(f32[2,2,16,128]{3,2,1,0:T(8,128)S(1)} %get-tuple-element.67), channel_id=1, source_target_pairs={{2,4},{3,5},{6,0},{7,1},{4,2},{5,3},{0,6},{1,7},{10,12},{11,13},{1... | collective-permute-start | bytes 98312 | tf_op jit(solution)/shard_map/ppermute | solution.py:83
  82.4 3.9 %collective-permute-start.16 = (f32[2,2,16,128]{3,2,1,0:T(8,128)S(1)}, f32[2,2,16,128]{3,2,1,0:T(8,128)S(1)}, u32[]{:S(2)}, u32[]{:S(2)}) collective-permute-start(f32[2,2,16,128]{3,2,1,0:T(8,128)S(1)} %get-tuple-element.68), channel_id=1, source_target_pairs={{0,2},{1,3},{4,6},{5,7},{2,0},{3,1},{6,4},{7,5},{8,10},{9,11},{12,... | collective-permute-start | bytes 98312 | tf_op jit(solution)/shard_map/ppermute | solution.py:83
  89.6 4.6 %collective-permute-start.19 = (bf16[2,2,16,256]{3,2,1,0:T(8,128)(2,1)S(1)}, bf16[2,2,16,256]{3,2,1,0:T(8,128)(2,1)S(1)}, u32[]{:S(2)}, u32[]{:S(2)}) collective-permute-start(bf16[2,2,16,256]{3,2,1,0:T(8,128)(2,1)S(1)} %get-tuple-element.72), channel_id=1, source_target_pairs={{1,2},{3,4},{5,6},{7,0},{2,1},{4,3},{6,5},{0,7},{9,10},{11,12},{13... | collective-permute-start | bytes 98312 | tf_op jit(solution)/shard_map/ppermute | solution.py:83
  90.3 3.9 %collective-permute-start.20 = (bf16[2,2,16,256]{3,2,1,0:T(8,128)(2,1)S(1)}, bf16[2,2,16,256]{3,2,1,0:T(8,128)(2,1)S(1)}, u32[]{:S(2)}, u32[]{:S(2)}) collective-permute-start(bf16[2,2,16,256]{3,2,1,0:T(8,128)(2,1)S(1)} %get-tuple-element.73), channel_id=1, source_target_pairs={{0,1},{2,3},{4,5},{6,7},{1,0},{3,2},{5,4},{7,6},{8,9},{10,11},{12,... | collective-permute-start | bytes 98312 | tf_op jit(solution)/shard_map/ppermute | solution.py:83
  96.1 16.8 %all-to-all-start.1 = ((f32[16,2,32,128]{3,2,1,0:T(8,128)}), f32[16,2,32,128]{3,2,1,0:T(8,128)S(1)}, u32[]{:S(2)}, u32[]{:S(2)}) async-start(f32[16,2,32,128]{3,2,1,0:T(8,128)} %shard_map.100), calls=%async_computation.1 | async-start | bytes 1048576 | tf_op jit(solution)/shard_map/all_to_all | solution.py:799
  102.3 9.1 %collective-permute-start.21 = (f32[2,16,128]{2,1,0:T(8,128)S(1)}, f32[2,16,128]{2,1,0:T(8,128)S(1)}, u32[]{:S(2)}, u32[]{:S(2)}) collective-permute-start(f32[2,16,128]{2,1,0:T(8,128)S(1)} %get-tuple-element.79), channel_id=1, source_target_pairs={{0,8},{8,0},{1,9},{9,1},{2,10},{10,2},{3,11},{11,3},{4,12},{12,4},... | collective-permute-start | bytes 49160 | tf_op jit(solution)/shard_map/ppermute | solution.py:88
